TPU v7x, 32 devices: a whole 2x2x4 slice. The times are simulated.
32 devices in a mesh: segment: 4 (over z), chan: 4 (over y, core), dp: 2 (over x).
Axes of the slice: x: 2, y: 2, z: 4, core: 2. Of those that a mesh axis runs over, the one named last changes fastest.
Arguments:
- grad_top: bfloat16 [2, 1536, 256], P('dp', None, 'chan'), may hold values from -6 to 6
- inputs_one: bfloat16 [4, 2, 1536, 256], P('segment', 'dp', 'chan'), may hold values from -6 to 6
- conv_one: bfloat16 [4, 2, 1536, 256], P('segment', 'dp', 'chan'), may hold values from -130 to 130
- inputs_two: bfloat16 [4, 2, 1536, 256], P('segment', 'dp', 'chan'), may hold values from -6 to 6
- conv_two: bfloat16 [4, 2, 1536, 256], P('segment', 'dp', 'chan'), may hold values from -130 to 130
- proj_weight: bfloat16 [4, 2, 1536, 1536], P('segment', None, 'chan'), may hold values from -0.15625 to 0.15625
- conv_weight: bfloat16 [4, 2, 1536, 432], P('segment', None, 'chan'), may hold values from -0.3125 to 0.3125
- norm_gain: float32 [4, 2, 1536], P('segment', None, 'chan'), may hold values from 0.1 to 1.9
- norm_bias: float32 [4, 2, 1536], P('segment', None, 'chan'), may hold values from -4 to 4
Outputs:
- grad_latent: bfloat16 [4, 2, 1536, 256], P('segment', 'dp', None, 'chan')
- grad_proj: float32 [4, 2, 1536, 1536], P('segment', None, 'chan')
- grad_conv: float32 [4, 2, 1536, 432], P('segment', None, 'chan')
- grad_gain: float32 [4, 2, 1536], P('segment', None, 'chan')
- grad_bias: float32 [4, 2, 1536], P('segment', None, 'chan')
All inputs are finite; a program needn't handle non-finite values.
Results may differ from a plain program's by a relative error of at most 0.009.
Values may be sent and summed in bfloat16 or wider, within the bound.
A program may use at most 64 MiB of HBM per device.

v0:
```python
import jax
import jax.numpy as jnp
from jax import lax
from jax.sharding import PartitionSpec as P

GS = 48
WW = 64


NORM_EPS = 1e-05


def passed_along(block, axis, distance):
    devices = range(lax.axis_size(axis))
    route = [(i - distance, i) for i in devices if i - distance in devices]
    return lax.ppermute(block, axis, route)


def shifted_cells(values, step_row, step_col, img_width):
    length = values.shape[2]
    margin = img_width + 1
    padded = jnp.pad(values, ((0, 0), (0, 0), (margin, margin)))
    start_at = margin + step_row * img_width + step_col
    part_view = lax.slice_in_dim(padded, start_at, start_at + length, axis=2)
    column = jnp.arange(length, dtype=jnp.int32) % img_width
    inside = (column + step_col >= 0) & (column + step_col < img_width)
    return jnp.where(inside, part_view, jnp.zeros((), values.dtype))


def norm_forward(saved_pre, gain_vec, bias_vec):
    chans, positions = saved_pre.shape
    groups_here = chans // GS
    pre = saved_pre.astype(jnp.float32).reshape(groups_here, GS, positions)
    centre = jnp.mean(pre, axis=(1, 2), keepdims=True)
    varied = jnp.mean(jnp.square(pre - centre), axis=(1, 2), keepdims=True)
    inv_std = lax.rsqrt(varied + NORM_EPS)
    normed = (pre - centre) * inv_std
    gain_grid = gain_vec.reshape(groups_here, GS, 1)
    scaled = normed * gain_grid + bias_vec.reshape(groups_here, GS, 1)
    gate_vals = jax.nn.sigmoid(scaled)
    act_bf = (scaled * gate_vals).astype(jnp.bfloat16).reshape(chans, positions)
    return (normed, scaled, gate_vals, inv_std, gain_grid, act_bf)


def conv_backward(grad_act, norm_state, saved_in, w_conv):
    normed, scaled, gate_vals, inv_std, gain_grid, act_bf = norm_state
    groups_here, _, positions = normed.shape
    chans = groups_here * GS
    grad_act = grad_act.reshape(groups_here, GS, positions)
    grad_norm = grad_act * (gate_vals * (1.0 + scaled * (1.0 - gate_vals)))
    gain_grad = jnp.sum(grad_norm * normed, axis=2).reshape(chans)
    bias_grad = jnp.sum(grad_norm, axis=2).reshape(chans)
    weighted = grad_norm * gain_grid
    first_mean = jnp.mean(weighted, axis=(1, 2), keepdims=True)
    second_mean = jnp.mean(weighted * normed, axis=(1, 2), keepdims=True)
    grad_pre = (inv_std * (weighted - first_mean - normed * second_mean)).astype(jnp.bfloat16)
    saved_grid = saved_in.reshape(groups_here, GS, positions)
    taps_w = w_conv.reshape(groups_here, GS, 9, GS)
    conv_parts = []
    back_sum = jnp.zeros((groups_here, GS, positions), jnp.float32)
    for tap_row in (-1, 0, 1):
        for tap_col in (-1, 0, 1):
            tap_at = 3 * (tap_row + 1) + tap_col + 1
            source = shifted_cells(saved_grid, tap_row, tap_col, WW)
            conv_parts.append(
                jnp.einsum("gop,gjp->goj", grad_pre, source, preferred_element_type=jnp.float32)
            )
            spread_back = jnp.einsum(
                "goj,gop->gjp",
                taps_w[:, :, tap_at, :],
                grad_pre,
                preferred_element_type=jnp.float32,
            )
            back_sum = back_sum + shifted_cells(spread_back, -tap_row, -tap_col, WW)
    conv_grad = jnp.stack(conv_parts, axis=2).reshape(chans, 9 * GS)
    branch = back_sum.reshape(chans, positions).astype(jnp.bfloat16)
    return (branch, conv_grad, gain_grad, bias_grad)


def block_sharded(grad_slab, saved_in, saved_pre, w_proj, w_conv, gain_vec, bias_vec):
    norm_state = norm_forward(saved_pre, gain_vec, bias_vec)
    act_bf = norm_state[5]
    grad_piece = lax.all_gather(grad_slab, "chan", axis=1, tiled=True)
    fresh = jnp.dot(w_proj, grad_piece, preferred_element_type=jnp.float32)
    weight_acc = lax.dot_general(
        act_bf, grad_piece, (((1,), (1,)), ((), ())), preferred_element_type=jnp.float32
    )
    branch, conv_grad, gain_grad, bias_grad = conv_backward(fresh, norm_state, saved_in, w_conv)
    returned = lax.all_to_all(branch, "chan", split_axis=1, concat_axis=0, tiled=True)
    out_slab = (grad_slab.astype(jnp.float32) + returned.astype(jnp.float32)).astype(jnp.bfloat16)
    return (out_slab, (weight_acc, conv_grad, gain_grad, bias_grad))


def take_micro(saved_all, index_at):
    return lax.dynamic_index_in_dim(saved_all[0], index_at, 0, keepdims=False)


def per_device(
    grad_top,
    inputs_one,
    conv_one,
    inputs_two,
    conv_two,
    proj_weight,
    conv_weight,
    norm_gain,
    norm_bias,
):
    segments = lax.axis_size("segment")
    segment_at = lax.axis_index("segment")
    local_mb = grad_top.shape[0]
    chans = conv_one.shape[2]
    width_all = proj_weight.shape[3]
    ticks = local_mb + segments - 1
    initial = (
        jnp.zeros(grad_top.shape[1:], jnp.bfloat16),
        jnp.zeros((1,) + grad_top.shape, jnp.bfloat16),
        jnp.zeros((2, chans, width_all), jnp.float32),
        jnp.zeros((2, chans, 9 * GS), jnp.float32),
        jnp.zeros((2, chans), jnp.float32),
        jnp.zeros((2, chans), jnp.float32),
    )

    def one_tick(tick_at, running):
        received, latent, proj_acc, conv_acc, gain_acc, bias_acc = running
        micro_at = tick_at - (segments - 1 - segment_at)
        is_valid = (micro_at >= 0) & (micro_at < local_mb)
        safe_mb = jnp.clip(micro_at, 0, local_mb - 1)
        top_grad = lax.dynamic_index_in_dim(grad_top, safe_mb, 0, keepdims=False)
        entering = jnp.where(segment_at == segments - 1, top_grad, received)
        mid_grad, grads_two = block_sharded(
            entering,
            take_micro(inputs_two, safe_mb),
            take_micro(conv_two, safe_mb),
            proj_weight[0, 1],
            conv_weight[0, 1],
            norm_gain[0, 1],
            norm_bias[0, 1],
        )
        out_grad, grads_one = block_sharded(
            mid_grad,
            take_micro(inputs_one, safe_mb),
            take_micro(conv_one, safe_mb),
            proj_weight[0, 0],
            conv_weight[0, 0],
            norm_gain[0, 0],
            norm_bias[0, 0],
        )
        weight_mask = is_valid.astype(jnp.float32)
        proj_acc = proj_acc + weight_mask * jnp.stack((grads_one[0], grads_two[0]))
        conv_acc = conv_acc + weight_mask * jnp.stack((grads_one[1], grads_two[1]))
        gain_acc = gain_acc + weight_mask * jnp.stack((grads_one[2], grads_two[2]))
        bias_acc = bias_acc + weight_mask * jnp.stack((grads_one[3], grads_two[3]))
        current = lax.dynamic_index_in_dim(latent[0], safe_mb, 0, keepdims=False)
        kept = jnp.where(is_valid, out_grad, current)
        latent = lax.dynamic_update_index_in_dim(latent, kept[None, None], safe_mb, 1)
        received = passed_along(out_grad, "segment", -1)
        return (received, latent, proj_acc, conv_acc, gain_acc, bias_acc)

    final = lax.fori_loop(0, ticks, one_tick, initial)
    latent = final[1]
    proj_sum, conv_sum, gain_sum, bias_sum = lax.psum(
        (final[2], final[3], final[4], final[5]), "dp"
    )
    return (latent, proj_sum[None], conv_sum[None], gain_sum[None], bias_sum[None])


def solution(mesh):
    return jax.shard_map(
        per_device,
        mesh=mesh,
        in_specs=(
            P("dp", None, "chan"),
            P("segment", "dp", "chan", None),
            P("segment", "dp", "chan", None),
            P("segment", "dp", "chan", None),
            P("segment", "dp", "chan", None),
            P("segment", None, "chan", None),
            P("segment", None, "chan", None),
            P("segment", None, "chan"),
            P("segment", None, "chan"),
        ),
        out_specs=(
            P("segment", "dp", None, "chan"),
            P("segment", None, "chan", None),
            P("segment", None, "chan", None),
            P("segment", None, "chan"),
            P("segment", None, "chan"),
        ),
        check_vma=False,
    )
```

profile of v0, /device:TPU:0, one launch (start us, length us, event | category | flops | bytes accessed | tf_op | source)
XLA Modules:
  0.0 624.5 jit_solution(14922544276449646448)
XLA Ops:
  10.2 452.6 %while.26 = (s32[]{:T(128)}, bf16[1536,64]{0,1:T(8,128)(2,1)S(1)}, bf16[1,1,1536,64]{2,3,1,0:T(8,128)(2,1)}, f32[2,384,1536]{2,1,0:T(8,128)}, f32[2,384,432]{1,2...) while((s32[]{:T(128)}, bf16[1536,64]{0,1:T(8,128)(2,1)S(1)}, ...), condition=%wide.region_21.22_spmd.clone, body=%wide.region_0.21_spmd.clone.sunk | while | flops 1570664192 | bytes 114773160 | solution.py:160
  19.8 10.1 %all_gather.24 = bf16[1536,256]{0,1:T(8,128)(2,1)S(1)} all-gather(bf16[1536,64]{0,1:T(8,128)(2,1)S(1)} %bitcast_select_fusion.3), channel_id=1, replica_groups=mesh['segment'=4,'chan'=4,'dp'=2] {'chan'}, dimensions={1}, use_global_device_ids=true | all-gather | bytes 983040 | tf_op jit(solution)/shard_map/while/body/eval_jaxpr/all_gather | solution.py:83
  37.1 4.0 all-to-all-start
  64.3 9.1 %all_gather.25 = bf16[1536,256]{0,1:T(8,128)(2,1)S(1)} all-gather(bf16[1536,64]{0,1:T(8,128)(2,1)S(1)} %add_convert_fusion.4), channel_id=1, replica_groups=mesh['segment'=4,'chan'=4,'dp'=2] {'chan'}, dimensions={1}, use_global_device_ids=true | all-gather | bytes 983040 | tf_op jit(solution)/shard_map/while/body/eval_jaxpr/all_gather | solution.py:83
  86.0 4.0 all-to-all-start.1
  100.9 2.8 copy.252
  105.7 5.0 fusion.357
  114.5 7.8 %collective-permute-done = bf16[1536,64]{0,1:T(8,128)(2,1)S(1)} collective-permute-done((bf16[1536,64]{0,1:T(8,128)(2,1)S(1)}, bf16[1536,64]{0,1:T(8,128)(2,1)S(1)}, u32[]{:S(2)}, u32[]{:S(2)}) %collective-permute-start) | collective-permute-done | bytes 196640 | tf_op jit(solution)/shard_map/while/body/eval_jaxpr/ppermute | solution.py:16
  131.9 8.8 %all_gather.24 = bf16[1536,256]{0,1:T(8,128)(2,1)S(1)} all-gather(bf16[1536,64]{0,1:T(8,128)(2,1)S(1)} %bitcast_select_fusion.3), channel_id=1, replica_groups=mesh['segment'=4,'chan'=4,'dp'=2] {'chan'}, dimensions={1}, use_global_device_ids=true | all-gather | bytes 983040 | tf_op jit(solution)/shard_map/while/body/eval_jaxpr/all_gather | solution.py:83
  147.9 4.0 all-to-all-start
  175.1 9.1 %all_gather.25 = bf16[1536,256]{0,1:T(8,128)(2,1)S(1)} all-gather(bf16[1536,64]{0,1:T(8,128)(2,1)S(1)} %add_convert_fusion.4), channel_id=1, replica_groups=mesh['segment'=4,'chan'=4,'dp'=2] {'chan'}, dimensions={1}, use_global_device_ids=true | all-gather | bytes 983040 | tf_op jit(solution)/shard_map/while/body/eval_jaxpr/all_gather | solution.py:83
  196.8 4.0 all-to-all-start.1
  211.7 2.8 copy.252
  216.5 6.4 %fusion.357 = f32[2,384,1536]{2,1,0:T(8,128)} fusion(f32[1,384,1536]{2,1,0:T(8,128)S(1)} %convolution_bitcast_fusion.72, f32[1,384,1536]{2,1,0:T(8,128)} %convolution_bitcast_fusion.73, f32[2,384,1536]{2,1,0:T(8,128)} %get-tuple-element.874, f32[]{:T(128)S(6)} %convert_element_type.432, pred[]{:T(512)S(6)} %compare.22), kind=kLoop, calls=%fused_computation.1.clone.1 | loop fusion | flops 4718592 | bytes 14155781 | tf_op jit(solution)/shard_map/while/body/eval_jaxpr/add | solution.py:150
  228.0 7.8 %collective-permute-done = bf16[1536,64]{0,1:T(8,128)(2,1)S(1)} collective-permute-done((bf16[1536,64]{0,1:T(8,128)(2,1)S(1)}, bf16[1536,64]{0,1:T(8,128)(2,1)S(1)}, u32[]{:S(2)}, u32[]{:S(2)}) %collective-permute-start) | collective-permute-done | bytes 196640 | tf_op jit(solution)/shard_map/while/body/eval_jaxpr/ppermute | solution.py:16
  245.4 8.8 %all_gather.24 = bf16[1536,256]{0,1:T(8,128)(2,1)S(1)} all-gather(bf16[1536,64]{0,1:T(8,128)(2,1)S(1)} %bitcast_select_fusion.3), channel_id=1, replica_groups=mesh['segment'=4,'chan'=4,'dp'=2] {'chan'}, dimensions={1}, use_global_device_ids=true | all-gather | bytes 983040 | tf_op jit(solution)/shard_map/while/body/eval_jaxpr/all_gather | solution.py:83
  261.4 4.0 all-to-all-start
  288.6 9.1 %all_gather.25 = bf16[1536,256]{0,1:T(8,128)(2,1)S(1)} all-gather(bf16[1536,64]{0,1:T(8,128)(2,1)S(1)} %add_convert_fusion.4), channel_id=1, replica_groups=mesh['segment'=4,'chan'=4,'dp'=2] {'chan'}, dimensions={1}, use_global_device_ids=true | all-gather | bytes 983040 | tf_op jit(solution)/shard_map/while/body/eval_jaxpr/all_gather | solution.py:83
  310.3 4.0 all-to-all-start.1
  325.2 2.8 copy.252
  330.0 6.4 %fusion.357 = f32[2,384,1536]{2,1,0:T(8,128)} fusion(f32[1,384,1536]{2,1,0:T(8,128)S(1)} %convolution_bitcast_fusion.72, f32[1,384,1536]{2,1,0:T(8,128)} %convolution_bitcast_fusion.73, f32[2,384,1536]{2,1,0:T(8,128)} %get-tuple-element.874, f32[]{:T(128)S(6)} %convert_element_type.432, pred[]{:T(512)S(6)} %compare.22), kind=kLoop, calls=%fused_computation.1.clone.1 | loop fusion | flops 4718592 | bytes 14155781 | tf_op jit(solution)/shard_map/while/body/eval_jaxpr/add | solution.py:150
  341.5 7.8 %collective-permute-done = bf16[1536,64]{0,1:T(8,128)(2,1)S(1)} collective-permute-done((bf16[1536,64]{0,1:T(8,128)(2,1)S(1)}, bf16[1536,64]{0,1:T(8,128)(2,1)S(1)}, u32[]{:S(2)}, u32[]{:S(2)}) %collective-permute-start) | collective-permute-done | bytes 196640 | tf_op jit(solution)/shard_map/while/body/eval_jaxpr/ppermute | solution.py:16
  358.9 8.8 %all_gather.24 = bf16[1536,256]{0,1:T(8,128)(2,1)S(1)} all-gather(bf16[1536,64]{0,1:T(8,128)(2,1)S(1)} %bitcast_select_fusion.3), channel_id=1, replica_groups=mesh['segment'=4,'chan'=4,'dp'=2] {'chan'}, dimensions={1}, use_global_device_ids=true | all-gather | bytes 983040 | tf_op jit(solution)/shard_map/while/body/eval_jaxpr/all_gather | solution.py:83
  374.9 4.0 all-to-all-start
  402.1 9.1 %all_gather.25 = bf16[1536,256]{0,1:T(8,128)(2,1)S(1)} all-gather(bf16[1536,64]{0,1:T(8,128)(2,1)S(1)} %add_convert_fusion.4), channel_id=1, replica_groups=mesh['segment'=4,'chan'=4,'dp'=2] {'chan'}, dimensions={1}, use_global_device_ids=true | all-gather | bytes 983040 | tf_op jit(solution)/shard_map/while/body/eval_jaxpr/all_gather | solution.py:83
  423.8 4.0 all-to-all-start.1
  438.7 2.8 copy.252
  443.5 6.4 %fusion.357 = f32[2,384,1536]{2,1,0:T(8,128)} fusion(f32[1,384,1536]{2,1,0:T(8,128)S(1)} %convolution_bitcast_fusion.72, f32[1,384,1536]{2,1,0:T(8,128)} %convolution_bitcast_fusion.73, f32[2,384,1536]{2,1,0:T(8,128)} %get-tuple-element.874, f32[]{:T(128)S(6)} %convert_element_type.432, pred[]{:T(512)S(6)} %compare.22), kind=kLoop, calls=%fused_computation.1.clone.1 | loop fusion | flops 4718592 | bytes 14155781 | tf_op jit(solution)/shard_map/while/body/eval_jaxpr/add | solution.py:150
  455.0 7.8 %collective-permute-done = bf16[1536,64]{0,1:T(8,128)(2,1)S(1)} collective-permute-done((bf16[1536,64]{0,1:T(8,128)(2,1)S(1)}, bf16[1536,64]{0,1:T(8,128)(2,1)S(1)}, u32[]{:S(2)}, u32[]{:S(2)}) %collective-permute-start) | collective-permute-done | bytes 196640 | tf_op jit(solution)/shard_map/while/body/eval_jaxpr/ppermute | solution.py:16
  463.5 5.5 all-reduce.18
  469.1 142.6 %all-reduce.22.cloned.1.call-done = (f32[1,2,384,1536]{3,2,1,0:T(8,128)}, f32[1,2,384,432]{2,3,1,0:T(8,128)}) async-done(((f32[1,2,384,1536]{3,2,1,0:T(8,128)}, f32[1,2,384,432]{2,3,1,0:T(8,128)}), (f32[1,2,384,1536]{3,2,1,0:T(8,128)}, f32[1,2,384,432]{2,3,1,0:T(8,128)})) %all-reduce.22.cloned.1.call-update) | async-done | bytes 6045712 | tf_op jit(solution)/shard_map/psum | solution.py:162
  611.6 4.9 copy.292
  (889 shorter events, 283.3 us)
Async XLA Ops:
  7.2 604.5 %all-reduce.22.cloned.1.call-start = ((), (), s32[]{:S(2)}) async-start(), calls=%async_computation.2 | async-start | bytes 12091392 | tf_op jit(solution)/shard_map/psum | solution.py:162
  14.2 15.7 %copy-start.20 = (f32[384]{0:T(512)}, f32[384]{0:T(512)S(1)}, u32[]{:S(2)}) copy-start(f32[384]{0:T(512)S(1)} %get-tuple-element.813) | copy-start | bytes 4612 | tf_op jit(solution)/shard_map/while
  18.3 11.6 %copy-start.22 = (f32[384]{0:T(512)S(1)}, f32[384]{0:T(512)}, u32[]{:S(2)}) copy-start(f32[384]{0:T(512)} %copy-done.21) | copy-start | bytes 4612 | tf_op jit(solution)/shard_map/while
  18.3 11.6 %copy-start.26 = (f32[384]{0:T(512)S(1)}, f32[384]{0:T(512)}, u32[]{:S(2)}) copy-start(f32[384]{0:T(512)} %mul.955) | copy-start | bytes 4612 | tf_op jit(solution)/shard_map/while
  18.3 11.6 %copy-start.42 = (bf16[1,2,384,1536]{3,2,1,0:T(8,128)(2,1)S(1)}, bf16[1,2,384,1536]{3,2,1,0:T(8,128)(2,1)}, u32[]{:S(2)}) copy-start(bf16[1,2,384,1536]{3,2,1,0:T(8,128)(2,1)} %get-tuple-element.902) | copy-start | bytes 7077892 | tf_op jit(solution)/shard_map/while
  37.1 24.4 %all-to-all-start = ((bf16[384,4,64]{0,2,1:T(8,128)(2,1)}), bf16[384,4,64]{0,2,1:T(8,128)(2,1)}, u32[]{:S(2)}, u32[]{:S(2)}) async-start(bf16[384,4,64]{0,2,1:T(8,128)(2,1)} %copy.245), calls=%async_computation | async-start | bytes 393216 | tf_op jit(solution)/shard_map/while/body/eval_jaxpr/all_to_all | solution.py:89
  61.5 11.9 %copy-start.27 = (f32[384]{0:T(512)S(1)}, f32[384]{0:T(512)}, u32[]{:S(2)}) copy-start(f32[384]{0:T(512)} %mul.953) | copy-start | bytes 4612 | tf_op jit(solution)/shard_map/while
  61.5 11.9 %copy-start.43 = (bf16[1,2,384,1536]{3,2,1,0:T(8,128)(2,1)S(1)}, bf16[1,2,384,1536]{3,2,1,0:T(8,128)(2,1)}, u32[]{:S(2)}) copy-start(bf16[1,2,384,1536]{3,2,1,0:T(8,128)(2,1)} %get-tuple-element.902) | copy-start | bytes 7077892 | tf_op jit(solution)/shard_map/while
  86.0 25.9 %all-to-all-start.1 = ((bf16[384,4,64]{0,2,1:T(8,128)(2,1)}), bf16[384,4,64]{0,2,1:T(8,128)(2,1)}, u32[]{:S(2)}, u32[]{:S(2)}) async-start(bf16[384,4,64]{0,2,1:T(8,128)(2,1)} %copy.249), calls=%async_computation.1 | async-start | bytes 393216 | tf_op jit(solution)/shard_map/while/body/eval_jaxpr/all_to_all | solution.py:89
  113.1 9.1 %collective-permute-start = (bf16[1536,64]{0,1:T(8,128)(2,1)S(1)}, bf16[1536,64]{0,1:T(8,128)(2,1)S(1)}, u32[]{:S(2)}, u32[]{:S(2)}) collective-permute-start(bf16[1536,64]{0,1:T(8,128)(2,1)S(1)} %get-tuple-element.842), channel_id=1, source_target_pairs={{8,0},{16,8},{24,16},{9,1},{17,9},{25,17},{10,2},{18,10},{26,18},{... | collective-permute-start | bytes 589832 | tf_op jit(solution)/shard_map/while/body/eval_jaxpr/ppermute | solution.py:16
  126.3 14.4 %copy-start.20 = (f32[384]{0:T(512)}, f32[384]{0:T(512)S(1)}, u32[]{:S(2)}) copy-start(f32[384]{0:T(512)S(1)} %get-tuple-element.813) | copy-start | bytes 4612 | tf_op jit(solution)/shard_map/while
  130.3 10.3 %copy-start.22 = (f32[384]{0:T(512)S(1)}, f32[384]{0:T(512)}, u32[]{:S(2)}) copy-start(f32[384]{0:T(512)} %copy-done.21) | copy-start | bytes 4612 | tf_op jit(solution)/shard_map/while
  130.4 10.3 %copy-start.26 = (f32[384]{0:T(512)S(1)}, f32[384]{0:T(512)}, u32[]{:S(2)}) copy-start(f32[384]{0:T(512)} %mul.955) | copy-start | bytes 4612 | tf_op jit(solution)/shard_map/while
  147.9 24.4 %all-to-all-start = ((bf16[384,4,64]{0,2,1:T(8,128)(2,1)}), bf16[384,4,64]{0,2,1:T(8,128)(2,1)}, u32[]{:S(2)}, u32[]{:S(2)}) async-start(bf16[384,4,64]{0,2,1:T(8,128)(2,1)} %copy.245), calls=%async_computation | async-start | bytes 393216 | tf_op jit(solution)/shard_map/while/body/eval_jaxpr/all_to_all | solution.py:89
  172.2 11.9 %copy-start.27 = (f32[384]{0:T(512)S(1)}, f32[384]{0:T(512)}, u32[]{:S(2)}) copy-start(f32[384]{0:T(512)} %mul.953) | copy-start | bytes 4612 | tf_op jit(solution)/shard_map/while
  172.3 11.9 %copy-start.43 = (bf16[1,2,384,1536]{3,2,1,0:T(8,128)(2,1)S(1)}, bf16[1,2,384,1536]{3,2,1,0:T(8,128)(2,1)}, u32[]{:S(2)}) copy-start(bf16[1,2,384,1536]{3,2,1,0:T(8,128)(2,1)} %get-tuple-element.902) | copy-start | bytes 7077892 | tf_op jit(solution)/shard_map/while
  196.8 28.6 %all-to-all-start.1 = ((bf16[384,4,64]{0,2,1:T(8,128)(2,1)}), bf16[384,4,64]{0,2,1:T(8,128)(2,1)}, u32[]{:S(2)}, u32[]{:S(2)}) async-start(bf16[384,4,64]{0,2,1:T(8,128)(2,1)} %copy.249), calls=%async_computation.1 | async-start | bytes 393216 | tf_op jit(solution)/shard_map/while/body/eval_jaxpr/all_to_all | solution.py:89
  226.6 9.1 %collective-permute-start = (bf16[1536,64]{0,1:T(8,128)(2,1)S(1)}, bf16[1536,64]{0,1:T(8,128)(2,1)S(1)}, u32[]{:S(2)}, u32[]{:S(2)}) collective-permute-start(bf16[1536,64]{0,1:T(8,128)(2,1)S(1)} %get-tuple-element.842), channel_id=1, source_target_pairs={{8,0},{16,8},{24,16},{9,1},{17,9},{25,17},{10,2},{18,10},{26,18},{... | collective-permute-start | bytes 589832 | tf_op jit(solution)/shard_map/while/body/eval_jaxpr/ppermute | solution.py:16
  239.8 14.4 %copy-start.20 = (f32[384]{0:T(512)}, f32[384]{0:T(512)S(1)}, u32[]{:S(2)}) copy-start(f32[384]{0:T(512)S(1)} %get-tuple-element.813) | copy-start | bytes 4612 | tf_op jit(solution)/shard_map/while
  243.9 10.3 %copy-start.22 = (f32[384]{0:T(512)S(1)}, f32[384]{0:T(512)}, u32[]{:S(2)}) copy-start(f32[384]{0:T(512)} %copy-done.21) | copy-start | bytes 4612 | tf_op jit(solution)/shard_map/while
  261.4 24.4 %all-to-all-start = ((bf16[384,4,64]{0,2,1:T(8,128)(2,1)}), bf16[384,4,64]{0,2,1:T(8,128)(2,1)}, u32[]{:S(2)}, u32[]{:S(2)}) async-start(bf16[384,4,64]{0,2,1:T(8,128)(2,1)} %copy.245), calls=%async_computation | async-start | bytes 393216 | tf_op jit(solution)/shard_map/while/body/eval_jaxpr/all_to_all | solution.py:89
  285.8 11.9 %copy-start.27 = (f32[384]{0:T(512)S(1)}, f32[384]{0:T(512)}, u32[]{:S(2)}) copy-start(f32[384]{0:T(512)} %mul.953) | copy-start | bytes 4612 | tf_op jit(solution)/shard_map/while
  285.8 11.9 %copy-start.43 = (bf16[1,2,384,1536]{3,2,1,0:T(8,128)(2,1)S(1)}, bf16[1,2,384,1536]{3,2,1,0:T(8,128)(2,1)}, u32[]{:S(2)}) copy-start(bf16[1,2,384,1536]{3,2,1,0:T(8,128)(2,1)} %get-tuple-element.902) | copy-start | bytes 7077892 | tf_op jit(solution)/shard_map/while
  310.3 28.6 %all-to-all-start.1 = ((bf16[384,4,64]{0,2,1:T(8,128)(2,1)}), bf16[384,4,64]{0,2,1:T(8,128)(2,1)}, u32[]{:S(2)}, u32[]{:S(2)}) async-start(bf16[384,4,64]{0,2,1:T(8,128)(2,1)} %copy.249), calls=%async_computation.1 | async-start | bytes 393216 | tf_op jit(solution)/shard_map/while/body/eval_jaxpr/all_to_all | solution.py:89
  340.1 9.1 %collective-permute-start = (bf16[1536,64]{0,1:T(8,128)(2,1)S(1)}, bf16[1536,64]{0,1:T(8,128)(2,1)S(1)}, u32[]{:S(2)}, u32[]{:S(2)}) collective-permute-start(bf16[1536,64]{0,1:T(8,128)(2,1)S(1)} %get-tuple-element.842), channel_id=1, source_target_pairs={{8,0},{16,8},{24,16},{9,1},{17,9},{25,17},{10,2},{18,10},{26,18},{... | collective-permute-start | bytes 589832 | tf_op jit(solution)/shard_map/while/body/eval_jaxpr/ppermute | solution.py:16
  353.3 14.4 %copy-start.20 = (f32[384]{0:T(512)}, f32[384]{0:T(512)S(1)}, u32[]{:S(2)}) copy-start(f32[384]{0:T(512)S(1)} %get-tuple-element.813) | copy-start | bytes 4612 | tf_op jit(solution)/shard_map/while
  357.4 10.3 %copy-start.22 = (f32[384]{0:T(512)S(1)}, f32[384]{0:T(512)}, u32[]{:S(2)}) copy-start(f32[384]{0:T(512)} %copy-done.21) | copy-start | bytes 4612 | tf_op jit(solution)/shard_map/while
  374.9 24.4 %all-to-all-start = ((bf16[384,4,64]{0,2,1:T(8,128)(2,1)}), bf16[384,4,64]{0,2,1:T(8,128)(2,1)}, u32[]{:S(2)}, u32[]{:S(2)}) async-start(bf16[384,4,64]{0,2,1:T(8,128)(2,1)} %copy.245), calls=%async_computation | async-start | bytes 393216 | tf_op jit(solution)/shard_map/while/body/eval_jaxpr/all_to_all | solution.py:89
  399.3 11.9 %copy-start.27 = (f32[384]{0:T(512)S(1)}, f32[384]{0:T(512)}, u32[]{:S(2)}) copy-start(f32[384]{0:T(512)} %mul.953) | copy-start | bytes 4612 | tf_op jit(solution)/shard_map/while
  399.3 11.9 %copy-start.43 = (bf16[1,2,384,1536]{3,2,1,0:T(8,128)(2,1)S(1)}, bf16[1,2,384,1536]{3,2,1,0:T(8,128)(2,1)}, u32[]{:S(2)}) copy-start(bf16[1,2,384,1536]{3,2,1,0:T(8,128)(2,1)} %get-tuple-element.902) | copy-start | bytes 7077892 | tf_op jit(solution)/shard_map/while
  423.8 28.6 %all-to-all-start.1 = ((bf16[384,4,64]{0,2,1:T(8,128)(2,1)}), bf16[384,4,64]{0,2,1:T(8,128)(2,1)}, u32[]{:S(2)}, u32[]{:S(2)}) async-start(bf16[384,4,64]{0,2,1:T(8,128)(2,1)} %copy.249), calls=%async_computation.1 | async-start | bytes 393216 | tf_op jit(solution)/shard_map/while/body/eval_jaxpr/all_to_all | solution.py:89
  453.6 9.1 %collective-permute-start = (bf16[1536,64]{0,1:T(8,128)(2,1)S(1)}, bf16[1536,64]{0,1:T(8,128)(2,1)S(1)}, u32[]{:S(2)}, u32[]{:S(2)}) collective-permute-start(bf16[1536,64]{0,1:T(8,128)(2,1)S(1)} %get-tuple-element.842), channel_id=1, source_target_pairs={{8,0},{16,8},{24,16},{9,1},{17,9},{25,17},{10,2},{18,10},{26,18},{... | collective-permute-start | bytes 589832 | tf_op jit(solution)/shard_map/while/body/eval_jaxpr/ppermute | solution.py:16
  (184 other events, 614.9 us)
Sparse Core Ops, SparseCore 0:
  463.0 148.6 all-reduce.21
where the time goes:
time: 628 us; the launch traced here: 624 us
  waiting for transfers between devices  174 us (28%)
  matrix products  132 us (21%)
  local copies, waits for them, and re-layouts  122 us (19%)
  blocking collectives  78.1 us (12%)
  other arithmetic  64.4 us (10%)
  starting transfers between devices  37.2 us (6%)
  between operations  14.1 us (2%)
    psum x1, waiting for transfers between devices, per_device(): lax.psum((final[2], final[3], final[4], final[5]), 'dp')  143 us
    dot_general x72, matrix products, conv_backward(): jnp.einsum('gop,gjp->goj', grad_pre, source, preferred_element_type=jnp.f...  77.1 us
    all_gather x8, blocking collectives, block_sharded(): grad_piece = lax.all_gather(grad_slab, 'chan', axis=1, tiled=True)  72.6 us
    dot_general x72, matrix products, conv_backward(): jnp.einsum('goj,gop->gjp', taps_w[:, :, tap_at, :], grad_pre, preferred_e...  33.4 us
    all_to_all x8, starting transfers between devices, block_sharded(): lax.all_to_all(branch, 'chan', split_axis=1, concat_axis=0, tiled=True)  32 us
    ppermute x4, waiting for transfers between devices, passed_along(): return lax.ppermute(block, axis, route)  31 us
    add x4, other arithmetic, one_tick(): proj_acc = proj_acc + weight_mask * jnp.stack((grads_one[0], grads_two[0]))  24.1 us
    another operation x8, local copies, waits for them, and re-layouts, conv_backward(): conv_grad = jnp.stack(conv_parts, axis=2).reshape(chans, 9 * GS)  20 us
  transfers between devices with their start and end apart: 13, of which 5 were waited for; matrix products, arithmetic and copies ran while one was open for 28% of the time, Pallas kernels for 0%

commit v1 on v0

v1 whole, which is shorter than its diff:
```python
import functools

import jax
import jax.numpy as jnp
from jax import lax
from jax.experimental import pallas as pl
from jax.experimental.pallas import tpu as pltpu
from jax.sharding import PartitionSpec as P

GS = 48
WW = 64
NORM_EPS = 1e-05
MESH = pl.DeviceIdType.MESH


def norm_forward(pre_t, gain, bias):
    positions, chans = pre_t.shape
    groups = chans // GS
    grid = pre_t.reshape(positions, groups, GS)
    centre = jnp.mean(grid, axis=(0, 2), keepdims=True)
    varied = jnp.mean(jnp.square(grid - centre), axis=(0, 2), keepdims=True)
    spread = lambda v: jnp.broadcast_to(v, (1, groups, GS)).reshape(1, chans)
    inv_std = spread(lax.rsqrt(varied + NORM_EPS))
    normed = (pre_t - spread(centre)) * inv_std
    scaled = normed * gain[None] + bias[None]
    gate = jax.nn.sigmoid(scaled)
    act = (scaled * gate).astype(jnp.bfloat16)
    slope = gate * (1.0 + scaled * (1.0 - gate))
    return normed, slope, inv_std, act


def chain_kernel(
    segments, n_chan, micro, gtop, wproj, wconv, gmat, slope, normed, gain, inv_std,
    ga_buf, gb_buf, gh_out, last_out, sums_out, taps,
    send_sems, recv_sems, relay_send, relay_recv,
):
    seg = lax.axis_index("segment")
    me = lax.axis_index("chan")
    pos, width = gh_out.shape[2:]
    chips = n_chan // 2
    core = lax.rem(me, 2)
    row = me // 2
    sibling = row * 2 + 1 - core
    peers = [lax.rem(row + d, chips) * 2 + core for d in range(1, chips)]

    barrier = pltpu.get_barrier_semaphore()
    for other in [sibling] + peers:
        pl.semaphore_signal(barrier, inc=1, device_id={"chan": other}, device_id_type=MESH)

    @pl.when(seg > 0)
    def _():
        pl.semaphore_signal(barrier, inc=1, device_id={"segment": seg - 1}, device_id_type=MESH)

    @pl.when(seg < segments - 1)
    def _():
        pl.semaphore_signal(barrier, inc=1, device_id={"segment": seg + 1}, device_id_type=MESH)

    linked = jnp.where(seg > 0, 1, 0) + jnp.where(seg < segments - 1, 1, 0)
    pl.semaphore_wait(barrier, chips + linked)

    taps[...] = jnp.zeros_like(taps)

    def push(buf, which, slot, piece, target):
        return pltpu.make_async_remote_copy(
            src_ref=buf.at[piece],
            dst_ref=buf.at[piece],
            send_sem=send_sems.at[which, slot],
            recv_sem=recv_sems.at[which, piece],
            device_id={"chan": target},
            device_id_type=MESH,
        )

    def gather(buf, which):
        started = [push(buf, which, 1 + d, me, peer) for d, peer in enumerate(peers)]
        started.append(push(buf, which, 0, me, sibling))
        for copy in started:
            copy.start()
        for d, peer in enumerate(peers):
            push(buf, which, 1 + d, peer, peer).wait_recv()
            hop = push(buf, which, chips + d, peer, sibling)
            hop.start()
            started.append(hop)
        push(buf, which, 0, sibling, sibling).wait_recv()
        for d in range(1, chips):
            piece = lax.rem(row + d, chips) * 2 + 1 - core
            push(buf, which, 0, piece, sibling).wait_recv()
        for copy in started:
            copy.wait_send()

    def relay(m):
        return pltpu.make_async_remote_copy(
            src_ref=last_out.at[m],
            dst_ref=ga_buf.at[m, me],
            send_sem=relay_send.at[m],
            recv_sem=relay_recv.at[m],
            device_id={"segment": lax.rem(seg + segments - 1, segments)},
            device_id_type=MESH,
        )

    column = lax.rem(lax.broadcasted_iota(jnp.int32, (pos, width), 0), WW)

    def block(m, b, buf):
        acc = jnp.zeros((pos, width), jnp.float32)
        for piece in range(n_chan):
            acc = acc + lax.dot_general(
                buf[piece], wproj[b, piece], (((1,), (1,)), ((), ())),
                preferred_element_type=jnp.float32,
            )
        xhat = normed[m, b]
        gn = acc * slope[m, b]
        bias_row = jnp.sum(gn, axis=0, keepdims=True)
        gain_row = jnp.sum(gn * xhat, axis=0, keepdims=True)
        sums_out[m, b, 0:1] = gain_row
        sums_out[m, b, 1:2] = bias_row
        gains = gain[b]
        lane = lax.broadcasted_iota(jnp.int32, (8, width), 0)
        pair = jnp.where(lane == 0, bias_row * gains, jnp.where(lane == 1, gain_row * gains, 0.0))
        means = jnp.dot(
            pair, gmat[...], precision=lax.Precision.HIGHEST, preferred_element_type=jnp.float32
        ) * (1.0 / (GS * pos))
        gh = inv_std[m, b] * (gn * gains - means[0:1] - xhat * means[1:2])
        gh = gh.astype(jnp.bfloat16)
        gh_out[m, b] = gh
        wide = gh.astype(jnp.float32)
        taps[0, WW:WW + pos] = jnp.where(
            column == WW - 1, 0.0, pltpu.roll(wide, pos - 1, 0)
        ).astype(jnp.bfloat16)
        taps[1, WW:WW + pos] = gh
        taps[2, WW:WW + pos] = jnp.where(
            column == 0, 0.0, pltpu.roll(wide, 1, 0)
        ).astype(jnp.bfloat16)
        back = jnp.zeros((pos, width), jnp.float32)
        for dr in range(3):
            start = WW - WW * (dr - 1)
            for dc in range(3):
                back = back + jnp.dot(
                    taps[dc, start:start + pos], wconv[b, 3 * dr + dc],
                    preferred_element_type=jnp.float32,
                )
        branch = back.astype(jnp.bfloat16).astype(jnp.float32)
        return (buf[me].astype(jnp.float32) + branch).astype(jnp.bfloat16)

    for m in range(micro):
        @pl.when(seg == segments - 1)
        def _():
            ga_buf[m] = gtop[m]

        @pl.when(seg < segments - 1)
        def _():
            relay(m).wait_recv()
            gather(ga_buf.at[m], 2 * m)

        gb_buf[m, me] = block(m, 1, ga_buf.at[m])
        gather(gb_buf.at[m], 2 * m + 1)
        last_out[m] = block(m, 0, gb_buf.at[m])

        @pl.when(seg > 0)
        def _():
            relay(m).start()

    for m in range(micro):
        @pl.when(seg > 0)
        def _():
            relay(m).wait_send()


def shifted(values, step_row, step_col):
    length = values.shape[-1]
    margin = WW + 1
    padded = jnp.pad(values, ((0, 0),) * (values.ndim - 1) + ((margin, margin),))
    start = margin + step_row * WW + step_col
    view = lax.slice_in_dim(padded, start, start + length, axis=values.ndim - 1)
    column = jnp.arange(length, dtype=jnp.int32) % WW
    inside = (column + step_col >= 0) & (column + step_col < WW)
    return jnp.where(inside, view, jnp.zeros((), values.dtype))


def per_device(
    segments, n_chan,
    grad_top, inputs_one, conv_one, inputs_two, conv_two,
    proj_weight, conv_weight, norm_gain, norm_bias,
):
    micro = grad_top.shape[0]
    width, pos = conv_one.shape[2:]
    groups = width // GS
    chans = proj_weight.shape[3]
    bf = jnp.bfloat16
    f32 = jnp.float32

    top = lax.all_gather(jnp.swapaxes(grad_top, 1, 2), "chan", axis=1, tiled=True)
    top = top.reshape(micro, pos, n_chan, width).transpose(0, 2, 1, 3)

    fwd = jax.vmap(jax.vmap(norm_forward), in_axes=(0, None, None))
    pre = jnp.stack((conv_one[0], conv_two[0]), axis=1)
    pre_t = jnp.swapaxes(pre, 2, 3).astype(f32)
    normed, slope, inv_std, act = fwd(pre_t, norm_gain[0], norm_bias[0])

    w_pieces = proj_weight[0].reshape(2, width, n_chan, width).transpose(0, 2, 1, 3)
    lane = jnp.arange(width)
    same = (lane[:, None] // GS) == (lane[None, :] // GS)
    taps_w = conv_weight[0].reshape(2, width, 9, GS).transpose(0, 2, 1, 3)
    w_diag = jnp.where(same, jnp.tile(taps_w, (1, 1, 1, groups)), jnp.zeros((), bf))

    vmem = pl.BlockSpec(memory_space=pltpu.VMEM)
    ga, gb, gh, last, sums = pl.pallas_call(
        functools.partial(chain_kernel, segments, n_chan, micro),
        out_shape=(
            jax.ShapeDtypeStruct((micro, n_chan, pos, width), bf),
            jax.ShapeDtypeStruct((micro, n_chan, pos, width), bf),
            jax.ShapeDtypeStruct((micro, 2, pos, width), bf),
            jax.ShapeDtypeStruct((micro, pos, width), bf),
            jax.ShapeDtypeStruct((micro, 2, 2, width), f32),
        ),
        in_specs=[vmem] * 8,
        out_specs=(vmem,) * 5,
        scratch_shapes=[
            pltpu.VMEM((3, pos + 2 * WW, width), bf),
            pltpu.SemaphoreType.DMA((2 * micro, n_chan)),
            pltpu.SemaphoreType.DMA((2 * micro, n_chan)),
            pltpu.SemaphoreType.DMA((micro,)),
            pltpu.SemaphoreType.DMA((micro,)),
        ],
        compiler_params=pltpu.CompilerParams(
            collective_id=0, has_side_effects=True, vmem_limit_bytes=56 * 1024 * 1024
        ),
    )(top, w_pieces, w_diag, same.astype(f32), slope, normed, norm_gain[0][:, None], inv_std)

    latent = lax.all_to_all(last, "chan", split_axis=1, concat_axis=2, tiled=True)
    latent = jnp.swapaxes(latent, 1, 2)[None]

    both = lambda v: lax.all_gather(v, "dp", axis=0, tiled=True)
    act_all = both(act)
    g_all = both(jnp.stack((gb, ga), axis=1))
    gh_all = both(gh)
    x_all = both(jnp.stack((inputs_one[0], inputs_two[0]), axis=1))
    n_all = act_all.shape[0]

    proj = jnp.einsum("mbpi,mbcpo->bico", act_all, g_all, preferred_element_type=f32)
    proj = proj.reshape(2, width, chans)
    x_grid = x_all.reshape(n_all, 2, groups, GS, pos)
    cols = jnp.stack(
        [shifted(x_grid, dr, dc) for dr in (-1, 0, 1) for dc in (-1, 0, 1)], axis=3
    ).reshape(n_all, 2, groups, 9 * GS, pos)
    gh_grid = jnp.swapaxes(gh_all, 2, 3).reshape(n_all, 2, groups, GS, pos)
    conv = jnp.einsum("mbgop,mbgkp->bgok", gh_grid, cols, preferred_element_type=f32)
    conv = conv.reshape(2, width, 9 * GS)
    sums = lax.psum(jnp.sum(sums, axis=0), "dp")
    return latent, proj[None], conv[None], sums[None, :, 0], sums[None, :, 1]


def solution(mesh):
    return jax.shard_map(
        functools.partial(per_device, mesh.shape["segment"], mesh.shape["chan"]),
        mesh=mesh,
        in_specs=(
            P("dp", None, "chan"),
            P("segment", "dp", "chan", None),
            P("segment", "dp", "chan", None),
            P("segment", "dp", "chan", None),
            P("segment", "dp", "chan", None),
            P("segment", None, "chan", None),
            P("segment", None, "chan", None),
            P("segment", None, "chan"),
            P("segment", None, "chan"),
        ),
        out_specs=(
            P("segment", "dp", None, "chan"),
            P("segment", None, "chan", None),
            P("segment", None, "chan", None),
            P("segment", None, "chan"),
            P("segment", None, "chan"),
        ),
        check_vma=False,
    )
```

time: 628 us -> 242 us (0.39)
  waiting for transfers between devices: 174 us -> 0.02 us
  matrix products: 132 us -> 7.87 us
  Pallas kernels: 0 us -> 99.7 us
  local copies, waits for them, and re-layouts: 122 us -> 35 us
  other arithmetic: 64.4 us -> 16 us
  starting transfers between devices: 37.2 us -> 3.41 us
  blocking collectives: 78.1 us -> 65.1 us
    psum x1 -> x0, waiting for transfers between devices: 143 us -> none  [per_device(): lax.psum((final[2], final[3], final[4], final[5]), 'dp')]
    dot_general x160 -> x2, matrix products: 132 us -> 7.87 us  [the longest x1 5.85 us: per_device(): jnp.einsum('mbpi,mbcpo->bico', act_all, g_all, preferred_element_type=f32)]
    pallas_call x0 -> x1, Pallas kernels: none -> 99.7 us  [per_device(): pl.pallas_call(functools.partial(chain_kernel, segments, n_chan, micro),...]
    add x12 -> x0, other arithmetic: 33.1 us -> none  [the longest x4 24.1 us: one_tick(): proj_acc = proj_acc + weight_mask * jnp.stack((grads_one[0], grads_two[0]))]
    ppermute x4 -> x0, waiting for transfers between devices: 31 us -> none  [passed_along(): return lax.ppermute(block, axis, route)]
    all_to_all x8 -> x1, starting transfers between devices: 32 us -> 3.37 us  [per_device(): lax.all_to_all(last, 'chan', split_axis=1, concat_axis=2, tiled=True)]
    slice x20 -> x0, local copies, waits for them, and re-layouts: 17.8 us -> none  [the longest x8 7.01 us: conv_backward(): taps_w[:, :, tap_at, :]]
    reshape x24 -> x1, local copies, waits for them, and re-layouts: 18.3 us -> 1.15 us  [per_device(): top = top.reshape(micro, pos, n_chan, width).transpose(0, 2, 1, 3)]
  transfers between devices with their start and end apart: 13 -> 2, of which waited for: 5 -> 0; matrix products, arithmetic and copies ran while one was open for 28% -> 5% of each run, Pallas kernels for 0% -> 0%
where the time goes in v1:
time: 242 us; the launch traced here: 241 us
  Pallas kernels  99.7 us (41%)
  blocking collectives  65.1 us (27%)
  local copies, waits for them, and re-layouts  35 us (14%)
  other arithmetic  16 us (7%)
  between operations  14.3 us (6%)
  matrix products  7.87 us (3%)
  starting transfers between devices  3.41 us (1%)
    pallas_call x1, Pallas kernels, per_device(): pl.pallas_call(functools.partial(chain_kernel, segments, n_chan, micro),...  99.7 us
    all_gather x3, blocking collectives, per_device(): both = lambda v: lax.all_gather(v, 'dp', axis=0, tiled=True)  49.7 us
    unnamed x25, local copies, waits for them, and re-layouts  15.4 us
    another operation x2, local copies, waits for them, and re-layouts, per_device(): jnp.tile(taps_w, (1, 1, 1, groups))  11.4 us
    all_gather x1, blocking collectives, per_device(): lax.all_gather(jnp.swapaxes(grad_top, 1, 2), 'chan', axis=1, tiled=True)  10.3 us
    dot_general x1, matrix products, per_device(): jnp.einsum('mbpi,mbcpo->bico', act_all, g_all, preferred_element_type=f32)  5.85 us
    select_n x1, other arithmetic, per_device(): jnp.where(same, jnp.tile(taps_w, (1, 1, 1, groups)), jnp.zeros((), bf))  5.65 us
    psum x1, blocking collectives, per_device(): sums = lax.psum(jnp.sum(sums, axis=0), 'dp')  5.11 us
  transfers between devices with their start and end apart: 2, of which 0 were waited for; matrix products, arithmetic and copies ran while one was open for 5% of the time, Pallas kernels for 0%

profile of v1, /device:TPU:0, one launch (start us, length us, event | category | flops | bytes accessed | tf_op | source)
XLA Modules:
  0.0 241.4 jit_solution(10483332666998126514)
XLA Ops:
  7.2 1.1 copy.143
  8.3 1.1 copy.142
  10.3 0.7 broadcast_in_dim.79.inv_std
  10.9 10.3 %all_gather.15 = bf16[1,256,1536]{2,1,0:T(8,128)(2,1)S(1)} all-gather(bf16[1,64,1536]{2,1,0:T(8,128)(2,1)} %bitcast.132), channel_id=1, replica_groups=mesh['segment'=4,'chan'=4,'dp'=2] {'chan'}, dimensions={1}, use_global_device_ids=true | all-gather | bytes 983040 | tf_op jit(solution)/shard_map/all_gather | solution.py:190
  21.5 1.2 copy.138
  22.6 3.0 %copy.139 = bf16[1,2,384,1536]{2,3,1,0:T(8,128)(2,1)S(1)} copy(bf16[1,2,384,1536]{3,2,1,0:T(8,128)(2,1)} %param.14) | data formatting | bytes 4718592 | tf_op args[5]
  25.7 2.6 %copy.140 = bf16[2,384,4,384]{3,1,2,0:T(8,128)(2,1)} copy(bf16[2,384,4,384]{1,3,2,0:T(8,128)(2,1)S(1)} %bitcast.118) | data formatting | bytes 4718592 | tf_op jit(solution)/shard_map/reshape;squeeze | solution.py:198
  28.3 2.8 %tile.4 = bf16[2,9,384,8,48]{2,4,3,1,0:T(8,128)(2,1)} broadcast(bf16[2,9,384,48]{2,3,1,0:T(8,128)(2,1)S(1)} %bitcast.130), dimensions={0,1,2,4} | broadcast | bytes 5971968 | tf_op jit(solution)/shard_map/tile | solution.py:202
  31.1 8.6 %copy.141 = bf16[2,9,384,384]{3,2,1,0:T(8,128)(2,1)} copy(bf16[2,9,384,384]{2,3,1,0:T(8,128)(2,1)} %bitcast.116) | data formatting | bytes 10616832 | tf_op jit(solution)/shard_map/tile | solution.py:202
  39.7 1.0 fusion.37
  40.7 0.6 broadcast_in_dim_squeeze.11.gain
  41.3 5.7 %broadcast_select_fusion.wconv = bf16[2,9,384,384]{3,2,1,0:T(8,128)(2,1)} fusion(bf16[2,9,384,384]{3,2,1,0:T(8,128)(2,1)} %copy.141, pred[384,384]{1,0:T(8,128)(4,1)S(1)} %get-tuple-element.51), kind=kLoop, calls=%fused_computation.2 | loop fusion | flops 2654208 | bytes 10764288 | tf_op jit(solution)/shard_map/jit(_where)/select_n | solution.py:202
  47.0 1.6 multiply_convert_fusion
  48.5 99.7 %shard_map.128 = (bf16[1,4,256,384]{3,2,1,0:T(8,128)(2,1)}, bf16[1,4,256,384]{3,2,1,0:T(8,128)(2,1)}, bf16[1,2,256,384]{3,2,1,0:T(8,128)(2,1)}, bf16[1,256,384]{2,1,0:T(8,128)(2,1)}, f32[1,2,2,384]{3,2,1,0:T(2,128)}) custom-call(bf16[1,4,256,384]{3,2,1,0:T(8,128)(2,1)} %bitcast.124, bf16[2,4,384,384]{3,2,1,0:T(8,128)(2,1)} %bitcast.119, ...), custom_call_target="tpu_custom_call" | custom-call | tf_op jit(solution)/shard_map/pallas_call | solution.py:205
  148.2 1.3 copy.205
  149.5 0.5 broadcast.152
  150.1 1.8 reduce.7
  151.9 0.7 reshape.146
  152.6 3.4 %all-to-all-start = ((bf16[4,2,12288]{2,1,0:T(2,128)(2,1)}), bf16[4,2,12288]{2,1,0:T(2,128)(2,1)S(1)}, u32[]{:S(2)}, u32[]{:S(2)}) async-start(bf16[4,2,12288]{2,1,0:T(2,128)(2,1)} %reshape.146), calls=%async_computation | async-start | bytes 393216 | tf_op jit(solution)/shard_map/all_to_all | solution.py:228
  156.0 2.7 %pad_maximum_fusion = bf16[1,2,4,256,384]{4,3,2,1,0:T(8,128)(2,1)} fusion(bf16[1,1,4,256,384]{4,3,2,1,0:T(8,128)(2,1)} %bitcast.128, bf16[1,1,4,256,384]{4,3,2,1,0:T(8,128)(2,1)} %bitcast.129), kind=kLoop, calls=%fused_computation.13 | loop fusion | flops 786432 | bytes 3145728 | tf_op jit(solution)/shard_map/stack | solution.py:233
  158.8 15.0 %all_gather.19 = bf16[2,2,384,256]{3,2,1,0:T(8,128)(2,1)S(1)} all-gather(bf16[1,2,384,256]{3,2,1,0:T(8,128)(2,1)S(1)} %pad_maximum_fusion.2), channel_id=1, replica_groups=mesh['segment'=4,'chan'=4,'dp'=2] {'dp'}, dimensions={0}, use_global_device_ids=true | all-gather | bytes 1179648 | tf_op jit(solution)/shard_map/all_gather | solution.py:231
  173.9 21.1 %all_gather.18 = bf16[2,2,256,384]{3,2,1,0:T(8,128)(2,1)S(1)} all-gather(bf16[1,2,256,384]{3,2,1,0:T(8,128)(2,1)S(1)} %copy-done.1), channel_id=1, replica_groups=mesh['segment'=4,'chan'=4,'dp'=2] {'dp'}, dimensions={0}, use_global_device_ids=true | all-gather | bytes 1179648 | tf_op jit(solution)/shard_map/all_gather | solution.py:231
  197.8 0.3 fusion.30
  198.1 2.0 fusion.4
  200.3 1.5 copy.161
  201.8 5.1 %psum.7 = f32[2,2,384]{2,1,0:T(2,128)S(1)} all-reduce(f32[2,2,384]{2,1,0:T(2,128)S(1)} %bitcast.134), channel_id=1, replica_groups=mesh['segment'=4,'chan'=4,'dp'=2] {'dp'}, use_global_device_ids=true, to_apply=%region_4.5 | all-reduce | flops 1536 | bytes 12288 | tf_op jit(solution)/shard_map/psum | solution.py:247
  206.9 0.6 copy.162
  207.5 0.6 copy.163
  208.1 13.6 %all_gather.16 = bf16[2,2,256,384]{3,2,1,0:T(8,128)(2,1)S(1)} all-gather(bf16[1,2,256,384]{3,2,1,0:T(8,128)(2,1)S(1)} %get-tuple-element.45), channel_id=1, replica_groups=mesh['segment'=4,'chan'=4,'dp'=2] {'dp'}, dimensions={0}, use_global_device_ids=true | all-gather | bytes 1179648 | tf_op jit(solution)/shard_map/all_gather | solution.py:231
  221.9 0.7 copy.174
  222.6 5.9 %fusion.2 = f32[2,384,4,384,1]{1,3,4,2,0:T(8,128)} fusion(bf16[2,2,4,256,384]{4,3,2,1,0:T(8,128)(2,1)} %all-gather.2.cloned.1.call-done, bf16[2,2,256,384]{3,2,1,0:T(8,128)(2,1)S(1)} %all_gather.16), kind=kOutput, calls=%fused_computation.3 | convolution fusion | flops 1207959552 | bytes 8650752 | tf_op jit(solution)/shard_map/mbpi,mbcpo->bico/dot_general | solution.py:238
  228.5 6.0 %copy.160 = f32[1,2,384,1536]{3,2,1,0:T(8,128)} copy(f32[1,2,384,1536]{2,3,1,0:T(8,128)} %bitcast.117) | data formatting | bytes 9437184
  (49 shorter events, 4.4 us)
Async XLA Ops:
  21.5 6.8 %copy-start = (bf16[1,2,384,432]{2,3,1,0:T(8,128)(2,1)S(1)}, bf16[1,2,384,432]{2,3,1,0:T(8,128)(2,1)}, u32[]{:S(2)}) copy-start(bf16[1,2,384,432]{2,3,1,0:T(8,128)(2,1)} %param.15) | copy-start | bytes 1990660
  31.1 9.6 %copy-start.4 = (f32[1,2,384]{2,1,0:T(2,128)S(1)}, f32[1,2,384]{2,1,0:T(2,128)}, u32[]{:S(2)}) copy-start(f32[1,2,384]{2,1,0:T(2,128)} %param.16) | copy-start | bytes 9220
  41.3 5.7 %copy-start.6 = (f32[1,2,384]{2,1,0:T(2,128)S(1)}, f32[1,2,384]{2,1,0:T(2,128)}, u32[]{:S(2)}) copy-start(f32[1,2,384]{2,1,0:T(2,128)} %param.17) | copy-start | bytes 9220
  148.2 10.6 %copy-start.2 = (bf16[1,1,384,256]{3,2,1,0:T(8,128)(2,1)S(1)}, bf16[1,1,384,256]{3,2,1,0:T(8,128)(2,1)}, u32[]{:S(2)}) copy-start(bf16[1,1,384,256]{3,2,1,0:T(8,128)(2,1)} %param.12) | copy-start | bytes 589828
  148.2 10.6 %copy-start.3 = (bf16[1,1,384,256]{3,2,1,0:T(8,128)(2,1)S(1)}, bf16[1,1,384,256]{3,2,1,0:T(8,128)(2,1)}, u32[]{:S(2)}) copy-start(bf16[1,1,384,256]{3,2,1,0:T(8,128)(2,1)} %param.10) | copy-start | bytes 589828
  148.2 25.6 %copy-start.1 = (bf16[1,2,256,384]{3,2,1,0:T(8,128)(2,1)S(1)}, bf16[1,2,256,384]{3,2,1,0:T(8,128)(2,1)}, u32[]{:S(2)}) copy-start(bf16[1,2,256,384]{3,2,1,0:T(8,128)(2,1)} %get-tuple-element.13) | copy-start | bytes 1179652
  152.6 69.1 %all-to-all-start = ((bf16[4,2,12288]{2,1,0:T(2,128)(2,1)}), bf16[4,2,12288]{2,1,0:T(2,128)(2,1)S(1)}, u32[]{:S(2)}, u32[]{:S(2)}) async-start(bf16[4,2,12288]{2,1,0:T(2,128)(2,1)} %reshape.146), calls=%async_computation | async-start | bytes 393216 | tf_op jit(solution)/shard_map/all_to_all | solution.py:228
  156.0 66.6 %all-gather.2.cloned.1.call-start = ((), (), s32[]{:S(2)}) async-start(), calls=%async_computation.1 | async-start | bytes 4718592 | tf_op jit(solution)/shard_map/all_gather | solution.py:231
  200.1 1.7 copy-start.5
Sparse Core Ops, SparseCore 0:
  158.9 57.7 all-gather.1

commit v2 on v1

v2 whole, which is shorter than its diff:
```python
import functools

import jax
import jax.numpy as jnp
from jax import lax
from jax.experimental import pallas as pl
from jax.experimental.pallas import tpu as pltpu
from jax.sharding import PartitionSpec as P

GS = 48
WW = 64
NORM_EPS = 1e-05
MESH = pl.DeviceIdType.MESH


def norm_forward(pre_t, gain, bias):
    positions, chans = pre_t.shape
    groups = chans // GS
    grid = pre_t.reshape(positions, groups, GS)
    centre = jnp.mean(grid, axis=(0, 2), keepdims=True)
    varied = jnp.mean(jnp.square(grid - centre), axis=(0, 2), keepdims=True)
    spread = lambda v: jnp.broadcast_to(v, (1, groups, GS)).reshape(1, chans)
    inv_std = spread(lax.rsqrt(varied + NORM_EPS))
    normed = (pre_t - spread(centre)) * inv_std
    scaled = normed * gain[None] + bias[None]
    gate = jax.nn.sigmoid(scaled)
    act = (scaled * gate).astype(jnp.bfloat16)
    slope = gate * (1.0 + scaled * (1.0 - gate))
    return normed, slope, inv_std, act


def chain_kernel(
    segments, n_chan, n_dp, gtop, wproj, wconv, same, slope, normed, gain, inv_std, act, saved,
    latent, proj, conv, sums,
    g_all, gh_all, act_all, x_all, sums_all, last, taps, x_taps, w_diag, gh_turned, square,
    send_sems, recv_sems, relay_send, relay_recv, dp_send, dp_recv,
    far_send, far_recv, hop_send, lat_send, lat_recv,
):
    seg = lax.axis_index("segment")
    me = lax.axis_index("chan")
    dp = lax.axis_index("dp")
    pos, width = last.shape
    part = pos // n_chan
    chips = n_chan // 2
    core = lax.rem(me, 2)
    row = me // 2
    sibling = row * 2 + 1 - core
    peers = [lax.rem(row + d, chips) * 2 + core for d in range(1, chips)]
    others = [lax.rem(me + d, n_chan) for d in range(1, n_chan)]
    replicas = [lax.rem(dp + d, n_dp) for d in range(1, n_dp)]
    top_seg = seg == segments - 1

    barrier = pltpu.get_barrier_semaphore()
    for other in others:
        pl.semaphore_signal(barrier, inc=1, device_id={"chan": other}, device_id_type=MESH)
    for other in replicas:
        pl.semaphore_signal(barrier, inc=1, device_id={"dp": other}, device_id_type=MESH)

    @pl.when(seg > 0)
    def _():
        pl.semaphore_signal(barrier, inc=1, device_id={"segment": seg - 1}, device_id_type=MESH)

    @pl.when(seg < segments - 1)
    def _():
        pl.semaphore_signal(barrier, inc=1, device_id={"segment": seg + 1}, device_id_type=MESH)

    linked = jnp.where(seg > 0, 1, 0) + jnp.where(seg < segments - 1, 1, 0)
    pl.semaphore_wait(barrier, n_chan - 1 + n_dp - 1 + linked)

    def whole(buf):
        return lambda piece: buf.at[piece]

    def strip(buf):
        return lambda piece: buf.at[:, pl.ds(pl.multiple_of(piece * part, part), part)]

    def push(view, which, slot, piece, target):
        return pltpu.make_async_remote_copy(
            src_ref=view(piece),
            dst_ref=view(piece),
            send_sem=send_sems.at[which, slot],
            recv_sem=recv_sems.at[which, piece],
            device_id={"chan": target},
            device_id_type=MESH,
        )

    def gather_start(view, which):
        started = [push(view, which, 1 + d, me, peer) for d, peer in enumerate(peers)]
        started.append(push(view, which, 0, me, sibling))
        for copy in started:
            copy.start()
        return started

    def gather_finish(view, which, started):
        for d, peer in enumerate(peers):
            push(view, which, 1 + d, peer, peer).wait_recv()
            hop = push(view, which, chips + d, peer, sibling)
            hop.start()
            started.append(hop)
        push(view, which, 0, sibling, sibling).wait_recv()
        for d in range(1, chips):
            piece = lax.rem(row + d, chips) * 2 + 1 - core
            push(view, which, 0, piece, sibling).wait_recv()
        for copy in started:
            copy.wait_send()

    def relay():
        return pltpu.make_async_remote_copy(
            src_ref=last,
            dst_ref=g_all.at[1, dp, me],
            send_sem=relay_send,
            recv_sem=relay_recv,
            device_id={"segment": lax.rem(seg + segments - 1, segments)},
            device_id_type=MESH,
        )

    def swap(kind, d, src, dst):
        target = replicas[d]
        return pltpu.make_async_remote_copy(
            src_ref=src,
            dst_ref=dst,
            send_sem=dp_send.at[kind, d],
            recv_sem=dp_recv.at[kind, dp],
            device_id={"dp": target},
            device_id_type=MESH,
        )

    def swap_start(kind, src, buf):
        for d in range(n_dp - 1):
            swap(kind, d, src, buf.at[dp]).start()

    def swap_finish(kind, src, buf):
        for d, other in enumerate(replicas):
            pltpu.make_async_remote_copy(
                src_ref=src,
                dst_ref=buf.at[other],
                send_sem=dp_send.at[kind, d],
                recv_sem=dp_recv.at[kind, other],
                device_id={"dp": other},
                device_id_type=MESH,
            ).wait()

    def far(b, d, j, source, piece):
        return pltpu.make_async_remote_copy(
            src_ref=g_all.at[b, source, piece],
            dst_ref=g_all.at[b, source, piece],
            send_sem=far_send.at[b, d, j],
            recv_sem=far_recv.at[b, source, piece],
            device_id={"dp": replicas[d]},
            device_id_type=MESH,
        )

    def hop(b, d, j, source, piece):
        return pltpu.make_async_remote_copy(
            src_ref=g_all.at[b, source, piece],
            dst_ref=g_all.at[b, source, piece],
            send_sem=hop_send.at[b, d, j],
            recv_sem=far_recv.at[b, source, piece],
            device_id={"chan": sibling},
            device_id_type=MESH,
        )

    def far_start(b):
        for d in range(n_dp - 1):
            for j, piece in enumerate([me] + peers):
                far(b, d, j, dp, piece).start()

    def far_pass(b):
        for d, other in enumerate(replicas):
            for j, piece in enumerate([me] + peers):
                far(b, d, j, other, piece).wait_recv()
                hop(b, d, j, other, piece).start()

    def far_finish(b):
        for d, other in enumerate(replicas):
            for j in range(chips):
                piece = lax.rem(row + j, chips) * 2 + 1 - core
                hop(b, d, j, other, piece).wait_recv()
            for j, piece in enumerate([me] + peers):
                far(b, d, j, dp, piece).wait_send()
                hop(b, d, j, other, piece).wait_send()

    column = lax.rem(lax.broadcasted_iota(jnp.int32, (pos, width), 0), WW)

    def side_by_side(values):
        wide = values.astype(jnp.float32)
        ahead = jnp.where(column == WW - 1, 0.0, pltpu.roll(wide, pos - 1, 0))
        behind = jnp.where(column == 0, 0.0, pltpu.roll(wide, 1, 0))
        return ahead.astype(jnp.bfloat16), behind.astype(jnp.bfloat16)

    def spread_taps(b):
        along = lax.broadcasted_iota(jnp.int32, (9 * GS, width), 0)
        within = lax.rem(lax.broadcasted_iota(jnp.int32, (9 * GS, width), 1), GS)
        for k in range(9):
            pick = jnp.where(along == within + k * GS, 1.0, 0.0).astype(jnp.bfloat16)
            tiled = jnp.dot(wconv[b], pick, preferred_element_type=jnp.float32)
            w_diag[b, k] = (tiled * same[...]).astype(jnp.bfloat16)

    def spread_inputs():
        swap_finish(0, act, act_all)
        swap_finish(1, saved, x_all)
        x_taps[...] = jnp.zeros_like(x_taps)
        for d in range(n_dp):
            for b in range(2):
                values = x_all[d, b]
                ahead, behind = side_by_side(values)
                x_taps[b, d, 0, WW:WW + pos] = behind
                x_taps[b, d, 1, WW:WW + pos] = values
                x_taps[b, d, 2, WW:WW + pos] = ahead

    def piece_of(b, piece):
        if width % 128 == 0:
            return wproj[b, :, piece * width:(piece + 1) * width]
        return wproj[b, piece]

    def block(b):
        acc = jnp.zeros((pos, width), jnp.float32)
        for piece in range(n_chan):
            acc = acc + lax.dot_general(
                g_all[b, dp, piece], piece_of(b, piece), (((1,), (1,)), ((), ())),
                preferred_element_type=jnp.float32,
            )
        xhat = normed[b]
        gn = acc * slope[b]
        bias_row = jnp.sum(gn, axis=0, keepdims=True)
        gain_row = jnp.sum(gn * xhat, axis=0, keepdims=True)
        sums_all[dp, b, 0:1] = gain_row
        sums_all[dp, b, 1:2] = bias_row
        gains = gain[b]
        lane = lax.broadcasted_iota(jnp.int32, (8, width), 0)
        pair = jnp.where(lane == 0, bias_row * gains, jnp.where(lane == 1, gain_row * gains, 0.0))
        means = jnp.dot(
            pair, same[...], precision=lax.Precision.HIGHEST, preferred_element_type=jnp.float32
        ) * (1.0 / (GS * pos))
        gh = inv_std[b] * (gn * gains - means[0:1] - xhat * means[1:2])
        gh = gh.astype(jnp.bfloat16)
        gh_all[b, dp] = gh
        ahead, behind = side_by_side(gh)
        taps[0, WW:WW + pos] = ahead
        taps[1, WW:WW + pos] = gh
        taps[2, WW:WW + pos] = behind
        back = jnp.zeros((pos, width), jnp.float32)
        for dr in range(3):
            start = WW - WW * (dr - 1)
            for dc in range(3):
                back = back + jnp.dot(
                    taps[dc, start:start + pos], w_diag[b, 3 * dr + dc],
                    preferred_element_type=jnp.float32,
                )
        branch = back.astype(jnp.bfloat16).astype(jnp.float32)
        return (g_all[b, dp, me].astype(jnp.float32) + branch).astype(jnp.bfloat16)

    def proj_grad(b):
        for piece in range(n_chan):
            acc = jnp.zeros((width, width), jnp.float32)
            for d in range(n_dp):
                acc = acc + jnp.dot(
                    act_all[d, b], g_all[b, d, piece], preferred_element_type=jnp.float32
                )
            if width % 128 == 0:
                proj[b, :, piece * width:(piece + 1) * width] = acc
            else:
                proj[b, piece] = acc

    def conv_grad(b):
        for d in range(n_dp):
            gh_turned[d] = gh_all[b, d].astype(jnp.float32).T.astype(jnp.bfloat16)
        for dr in range(3):
            start = WW * dr
            for dc in range(3):
                at = (3 * dr + dc) * GS
                acc = jnp.zeros((width, width), jnp.float32)
                for d in range(n_dp):
                    acc = acc + jnp.dot(
                        gh_turned[d], x_taps[b, d, dc, start:start + pos],
                        preferred_element_type=jnp.float32,
                    )
                square[...] = acc
                for q in range(0, width, GS):
                    conv[b, q:q + GS, at:at + GS] = square[q:q + GS, q:q + GS]

    act_all[dp] = act[...]
    x_all[dp] = saved[...]
    taps[...] = jnp.zeros_like(taps)
    entering = g_all.at[1, dp]
    middle = g_all.at[0, dp]

    @pl.when(top_seg)
    def _():
        entering[:, pl.ds(pl.multiple_of(me * part, part), part)] = gtop[...]
        started = gather_start(strip(entering), 1)
        spread_taps(1)
        gather_finish(strip(entering), 1, started)
        swap_start(0, act, act_all)
        swap_start(1, saved, x_all)

    @pl.when(seg < segments - 1)
    def _():
        swap_start(0, act, act_all)
        swap_start(1, saved, x_all)
        spread_taps(1)
        spread_taps(0)
        spread_inputs()
        relay().wait_recv()
        gather_finish(whole(entering), 1, gather_start(whole(entering), 1))

    far_start(1)
    middle[me] = block(1)
    started = gather_start(whole(middle), 0)
    swap_start(2, gh_all.at[1, dp], gh_all.at[1])

    @pl.when(top_seg)
    def _():
        spread_taps(0)

    gather_finish(whole(middle), 0, started)
    far_start(0)
    last[...] = block(0)

    @pl.when(seg > 0)
    def _():
        relay().start()

    swap_start(3, gh_all.at[0, dp], gh_all.at[0])
    swap_start(4, sums_all.at[dp], sums_all)
    for d, other in enumerate(others):
        pltpu.make_async_remote_copy(
            src_ref=last.at[pl.ds(pl.multiple_of(other * part, part), part)],
            dst_ref=latent.at[me],
            send_sem=lat_send.at[d],
            recv_sem=lat_recv.at[me],
            device_id={"chan": other},
            device_id_type=MESH,
        ).start()
    latent[me] = last[pl.ds(pl.multiple_of(me * part, part), part)]

    @pl.when(top_seg)
    def _():
        spread_inputs()

    far_pass(1)
    swap_finish(2, gh_all.at[1, dp], gh_all.at[1])
    conv_grad(1)
    far_pass(0)
    far_finish(1)
    proj_grad(1)
    far_finish(0)
    proj_grad(0)
    swap_finish(3, gh_all.at[0, dp], gh_all.at[0])
    conv_grad(0)
    swap_finish(4, sums_all.at[dp], sums_all)
    total = sums_all[0]
    for d in range(1, n_dp):
        total = total + sums_all[d]
    sums[...] = total
    for d, other in enumerate(others):
        pltpu.make_async_remote_copy(
            src_ref=last.at[pl.ds(pl.multiple_of(other * part, part), part)],
            dst_ref=latent.at[other],
            send_sem=lat_send.at[d],
            recv_sem=lat_recv.at[other],
            device_id={"chan": other},
            device_id_type=MESH,
        ).wait()

    @pl.when(seg > 0)
    def _():
        relay().wait_send()


def per_device(
    segments, n_chan, n_dp,
    grad_top, inputs_one, conv_one, inputs_two, conv_two,
    proj_weight, conv_weight, norm_gain, norm_bias,
):
    width, pos = conv_one.shape[2:]
    part = pos // n_chan
    chans = proj_weight.shape[3]
    bf = jnp.bfloat16
    f32 = jnp.float32

    top = grad_top.reshape(n_chan, width, part).swapaxes(1, 2)
    pre = jnp.concatenate((conv_one[0], conv_two[0]), axis=0)
    pre_t = jnp.swapaxes(pre, 1, 2).astype(f32)
    normed, slope, inv_std, act = jax.vmap(norm_forward)(pre_t, norm_gain[0], norm_bias[0])
    act = jnp.swapaxes(act, 1, 2)
    saved = jnp.swapaxes(jnp.concatenate((inputs_one[0], inputs_two[0]), axis=0), 1, 2)
    lane = jnp.arange(width)
    same = ((lane[:, None] // GS) == (lane[None, :] // GS)).astype(f32)
    w_proj = proj_weight[0]
    proj_shape = (2, width, chans)
    if width % 128:
        w_proj = w_proj.reshape(2, width, n_chan, width).swapaxes(1, 2)
        proj_shape = (2, n_chan, width, width)

    vmem = pl.BlockSpec(memory_space=pltpu.VMEM)
    dma = pltpu.SemaphoreType.DMA
    chips = n_chan // 2
    apart = max(n_dp - 1, 1)
    latent, proj, conv, sums = pl.pallas_call(
        functools.partial(chain_kernel, segments, n_chan, n_dp),
        out_shape=(
            jax.ShapeDtypeStruct((n_chan, part, width), bf),
            jax.ShapeDtypeStruct(proj_shape, f32),
            jax.ShapeDtypeStruct((2, width, 9 * GS), f32),
            jax.ShapeDtypeStruct((2, 2, width), f32),
        ),
        in_specs=[vmem] * 10,
        out_specs=(vmem,) * 4,
        scratch_shapes=[
            pltpu.VMEM((2, n_dp, n_chan, pos, width), bf),
            pltpu.VMEM((2, n_dp, pos, width), bf),
            pltpu.VMEM((n_dp, 2, width, pos), bf),
            pltpu.VMEM((n_dp, 2, pos, width), bf),
            pltpu.VMEM((n_dp, 2, 2, width), f32),
            pltpu.VMEM((pos, width), bf),
            pltpu.VMEM((3, pos + 2 * WW, width), bf),
            pltpu.VMEM((2, n_dp, 3, pos + 2 * WW, width), bf),
            pltpu.VMEM((2, 9, width, width), bf),
            pltpu.VMEM((n_dp, width, pos), bf),
            pltpu.VMEM((width, width), f32),
            dma((2, n_chan)),
            dma((2, n_chan)),
            dma,
            dma,
            dma((5, apart)),
            dma((5, n_dp)),
            dma((2, apart, chips)),
            dma((2, n_dp, n_chan)),
            dma((2, apart, chips)),
            dma((n_chan,)),
            dma((n_chan,)),
        ],
        compiler_params=pltpu.CompilerParams(
            collective_id=0, has_side_effects=True, vmem_limit_bytes=60 * 1024 * 1024
        ),
    )(top, w_proj, conv_weight[0], same, slope, normed, norm_gain[0][:, None], inv_std, act, saved)

    latent = jnp.swapaxes(latent, 1, 2).reshape(1, 1, chans, part)
    if width % 128:
        proj = proj.swapaxes(1, 2).reshape(2, width, chans)
    return latent, proj[None], conv[None], sums[None, :, 0], sums[None, :, 1]


def solution(mesh):
    return jax.shard_map(
        functools.partial(
            per_device, mesh.shape["segment"], mesh.shape["chan"], mesh.shape["dp"]
        ),
        mesh=mesh,
        in_specs=(
            P("dp", None, "chan"),
            P("segment", "dp", "chan", None),
            P("segment", "dp", "chan", None),
            P("segment", "dp", "chan", None),
            P("segment", "dp", "chan", None),
            P("segment", None, "chan", None),
            P("segment", None, "chan", None),
            P("segment", None, "chan"),
            P("segment", None, "chan"),
        ),
        out_specs=(
            P("segment", "dp", None, "chan"),
            P("segment", None, "chan", None),
            P("segment", None, "chan", None),
            P("segment", None, "chan"),
            P("segment", None, "chan"),
        ),
        check_vma=False,
    )
```

time: 242 us -> 155 us (0.64)
  blocking collectives: 65.1 us -> 0 us
  Pallas kernels: 99.7 us -> 127 us
  local copies, waits for them, and re-layouts: 35 us -> 21.3 us
  between operations: 14.3 us -> 0.74 us
  other arithmetic: 16 us -> 6.35 us
  matrix products: 7.87 us -> 0 us
  starting transfers between devices: 3.41 us -> 0 us
    all_gather x4 -> x0, blocking collectives: 60 us -> none  [the longest x3 49.7 us: per_device(): both = lambda v: lax.all_gather(v, 'dp', axis=0, tiled=True)]
    pallas_call x1, Pallas kernels: 99.7 us -> 127 us  [per_device(): pl.pallas_call(functools.partial(chain_kernel, segments, n_chan, n_dp), o...]
    another operation x4 -> x1, local copies, waits for them, and re-layouts: 14.6 us -> 1.27 us  [norm_forward(): scaled = normed * gain[None] + bias[None]]
    dot_general x2 -> x0, matrix products: 7.87 us -> none  [the longest x1 5.85 us: per_device(): jnp.einsum('mbpi,mbcpo->bico', act_all, g_all, preferred_element_type=f32)]
    select_n x2 -> x1, other arithmetic: 5.66 us -> 0.01 us  [per_device(): same = (lane[:, None] // GS == lane[None, :] // GS).astype(f32)]
    psum x1 -> x0, blocking collectives: 5.11 us -> none  [per_device(): sums = lax.psum(jnp.sum(sums, axis=0), 'dp')]
    unnamed x9 -> x0, other arithmetic: 4.3 us -> none
    all_to_all x1 -> x0, starting transfers between devices: 3.37 us -> none  [per_device(): lax.all_to_all(last, 'chan', split_axis=1, concat_axis=2, tiled=True)]
  transfers between devices with their start and end apart: 2 -> 0, of which waited for: 0 -> 0; matrix products, arithmetic and copies ran while one was open for 5% -> 0% of each run, Pallas kernels for 0% -> 0%
where the time goes in v2:
time: 155 us
  Pallas kernels  127 us (82%)
  local copies, waits for them, and re-layouts  21.3 us (14%)
  other arithmetic  6.35 us (4%)
    pallas_call x1, Pallas kernels, per_device(): pl.pallas_call(functools.partial(chain_kernel, segments, n_chan, n_dp), o...  127 us
    unnamed x17, local copies, waits for them, and re-layouts  12.3 us

profile of v2, /device:TPU:0, one launch (start us, length us, event | category | flops | bytes accessed | tf_op | source)
XLA Modules:
  0.0 155.0 jit_solution(8643423896690273838)
XLA Ops:
  0.6 0.0 copy-start.3
  0.7 1.3 fusion.1
  2.0 1.3 broadcast_in_dim_squeeze.11.gain
  3.3 0.1 reduce_sum.24
  3.3 0.1 reduce_sum.25
  3.4 0.1 broadcast_in_dim.26
  3.5 0.1 broadcast_in_dim.27
  3.6 1.3 fusion.4
  4.9 0.1 reduce_sum.36
  5.0 0.1 reduce_sum.37
  5.1 0.1 broadcast_in_dim.28
  5.2 0.1 broadcast_in_dim.29
  5.3 0.7 broadcast_in_dim.30.inv_std
  5.9 1.0 reshape.91
  6.9 0.7 copy.43
  7.6 1.1 copy.34
  8.7 1.1 copy.35
  9.8 0.8 maximum_bitcast_fusion.saved
  10.7 1.3 fusion.13.act
  11.9 0.9 compare_convert_fusion.same
  12.9 1.2 copy.33
  14.0 0.5 fusion.2
  14.5 1.2 copy.37.normed
  15.7 1.1 copy.36.slope
  16.8 126.6 %shard_map.128 = (bf16[4,64,384]{2,1,0:T(8,128)(2,1)}, f32[2,384,1536]{2,1,0:T(8,128)}, f32[2,384,432]{2,1,0:T(8,128)}, f32[2,2,384]{2,1,0:T(2,128)}) custom-call(bf16[4,64,384]{2,1,0:T(8,128)(2,1)} %bitcast.50, bf16[2,384,1536]{2,1,0:T(8,128)(2,1)} %bitcast.48, bf16[2,384,432]{2,1,0:T(8,128)(2,1)} %bitcast.39, f32[384,384]{1,0:T(8,128)} %compare_convert_fusion.same, ...), custom_call_target="tpu_custom_call" | custom-call | tf_op jit(solution)/shard_map/pallas_call | solution.py:399
  143.4 1.1 copy.38
  144.5 0.8 reshape.92
  145.3 0.8 slice_bitcast_fusion
  146.0 0.6 copy.41
  146.6 0.6 copy.40
  147.2 2.9 %copy.39 = f32[1,2,384,432]{2,3,1,0:T(8,128)} copy(f32[1,2,384,432]{3,2,1,0:T(8,128)} %bitcast.49) | data formatting | bytes 2654208
  150.1 4.8 %copy.45 = f32[1,2,384,1536]{3,2,1,0:T(8,128)} copy(f32[1,2,384,1536]{3,2,1,0:T(8,128)} %bitcast.38) | data formatting | bytes 9437184
  (12 shorter events, 0.0 us)
Async XLA Ops:
  0.6 10.0 %copy-start.3 = (f32[1,2,384]{2,1,0:T(2,128)S(1)}, f32[1,2,384]{2,1,0:T(2,128)}, u32[]{:S(2)}) copy-start(f32[1,2,384]{2,1,0:T(2,128)} %param.16) | copy-start | bytes 9220
  0.6 10.0 %copy-start.4 = (f32[1,2,384]{2,1,0:T(2,128)S(1)}, f32[1,2,384]{2,1,0:T(2,128)}, u32[]{:S(2)}) copy-start(f32[1,2,384]{2,1,0:T(2,128)} %param.17) | copy-start | bytes 9220
  0.7 12.2 %copy-start.2 = (bf16[1,2,384,432]{2,3,1,0:T(8,128)(2,1)S(1)}, bf16[1,2,384,432]{2,3,1,0:T(8,128)(2,1)}, u32[]{:S(2)}) copy-start(bf16[1,2,384,432]{2,3,1,0:T(8,128)(2,1)} %param.15) | copy-start | bytes 1990660
  0.7 10.0 %copy-start = (bf16[1,1,384,256]{3,2,1,0:T(8,128)(2,1)S(1)}, bf16[1,1,384,256]{3,2,1,0:T(8,128)(2,1)}, u32[]{:S(2)}) copy-start(bf16[1,1,384,256]{3,2,1,0:T(8,128)(2,1)} %param.13) | copy-start | bytes 589828
  0.7 10.0 %copy-start.1 = (bf16[1,1,384,256]{3,2,1,0:T(8,128)(2,1)S(1)}, bf16[1,1,384,256]{3,2,1,0:T(8,128)(2,1)}, u32[]{:S(2)}) copy-start(bf16[1,1,384,256]{3,2,1,0:T(8,128)(2,1)} %param.11) | copy-start | bytes 589828

commit v3 on v2

--- a/solution.py
+++ b/solution.py
@@ -13,26 +13,11 @@
 MESH = pl.DeviceIdType.MESH
 
 
-def norm_forward(pre_t, gain, bias):
-    positions, chans = pre_t.shape
-    groups = chans // GS
-    grid = pre_t.reshape(positions, groups, GS)
-    centre = jnp.mean(grid, axis=(0, 2), keepdims=True)
-    varied = jnp.mean(jnp.square(grid - centre), axis=(0, 2), keepdims=True)
-    spread = lambda v: jnp.broadcast_to(v, (1, groups, GS)).reshape(1, chans)
-    inv_std = spread(lax.rsqrt(varied + NORM_EPS))
-    normed = (pre_t - spread(centre)) * inv_std
-    scaled = normed * gain[None] + bias[None]
-    gate = jax.nn.sigmoid(scaled)
-    act = (scaled * gate).astype(jnp.bfloat16)
-    slope = gate * (1.0 + scaled * (1.0 - gate))
-    return normed, slope, inv_std, act
-
-
 def chain_kernel(
-    segments, n_chan, n_dp, gtop, wproj, wconv, same, slope, normed, gain, inv_std, act, saved,
+    segments, n_chan, n_dp, gtop, wproj, wconv, gain, bias, pre_one, pre_two, in_one, in_two,
     latent, proj, conv, sums,
     g_all, gh_all, act_all, x_all, sums_all, last, taps, x_taps, w_diag, gh_turned, square,
+    same, slope, normed, inv_std, act, saved, w_turned,
     send_sems, recv_sems, relay_send, relay_recv, dp_send, dp_recv,
     far_send, far_recv, hop_send, lat_send, lat_recv,
 ):
@@ -40,6 +25,7 @@
     me = lax.axis_index("chan")
     dp = lax.axis_index("dp")
     pos, width = last.shape
+    half = width // 2
     part = pos // n_chan
     chips = n_chan // 2
     core = lax.rem(me, 2)
@@ -193,7 +179,38 @@
         for k in range(9):
             pick = jnp.where(along == within + k * GS, 1.0, 0.0).astype(jnp.bfloat16)
             tiled = jnp.dot(wconv[b], pick, preferred_element_type=jnp.float32)
-            w_diag[b, k] = (tiled * same[...]).astype(jnp.bfloat16)
+            tiled = tiled * same[...]
+            for h in range(2):
+                side = slice(h * half, (h + 1) * half)
+                w_diag[b, k, h] = tiled[side, side].astype(jnp.bfloat16)
+
+    def group_mean(rows):
+        return jnp.dot(
+            rows, same[...], precision=lax.Precision.HIGHEST, preferred_element_type=jnp.float32
+        ) * (1.0 / (GS * pos))
+
+    def column_sum(values):
+        return jnp.broadcast_to(jnp.sum(values, axis=0, keepdims=True), (8, width))
+
+    def norm_forward(b):
+        pre = (pre_one, pre_two)[b][...].astype(jnp.float32).T
+        apart = pre - group_mean(column_sum(pre))[0:1]
+        inv = lax.rsqrt(group_mean(column_sum(apart * apart))[0:1] + NORM_EPS)
+        xhat = apart * inv
+        n = xhat * gain[b:b + 1] + bias[b:b + 1]
+        gate = jax.nn.sigmoid(n)
+        inv_std[b] = inv
+        normed[b] = xhat
+        slope[b] = gate * (1.0 + n * (1.0 - gate))
+        act[b] = (n * gate).T.astype(jnp.bfloat16)
+        for piece in range(n_chan):
+            w_turned[b, piece] = piece_of(b, piece).astype(jnp.float32).T.astype(jnp.bfloat16)
+
+    def inputs_start():
+        act_all[dp] = act[...]
+        x_all[dp] = saved[...]
+        swap_start(0, act, act_all)
+        swap_start(1, saved, x_all)
 
     def spread_inputs():
         swap_finish(0, act, act_all)
@@ -201,7 +218,7 @@
         x_taps[...] = jnp.zeros_like(x_taps)
         for d in range(n_dp):
             for b in range(2):
-                values = x_all[d, b]
+                values = x_all[d, b].astype(jnp.float32).T.astype(jnp.bfloat16)
                 ahead, behind = side_by_side(values)
                 x_taps[b, d, 0, WW:WW + pos] = behind
                 x_taps[b, d, 1, WW:WW + pos] = values
@@ -216,7 +233,7 @@
         acc = jnp.zeros((pos, width), jnp.float32)
         for piece in range(n_chan):
             acc = acc + lax.dot_general(
-                g_all[b, dp, piece], piece_of(b, piece), (((1,), (1,)), ((), ())),
+                g_all[b, dp, piece], w_turned[b, piece], (((1,), (0,)), ((), ())),
                 preferred_element_type=jnp.float32,
             )
         xhat = normed[b]
@@ -225,27 +242,29 @@
         gain_row = jnp.sum(gn * xhat, axis=0, keepdims=True)
         sums_all[dp, b, 0:1] = gain_row
         sums_all[dp, b, 1:2] = bias_row
-        gains = gain[b]
+        gains = gain[b:b + 1]
         lane = lax.broadcasted_iota(jnp.int32, (8, width), 0)
         pair = jnp.where(lane == 0, bias_row * gains, jnp.where(lane == 1, gain_row * gains, 0.0))
-        means = jnp.dot(
-            pair, same[...], precision=lax.Precision.HIGHEST, preferred_element_type=jnp.float32
-        ) * (1.0 / (GS * pos))
+        means = group_mean(pair)
         gh = inv_std[b] * (gn * gains - means[0:1] - xhat * means[1:2])
         gh = gh.astype(jnp.bfloat16)
         gh_all[b, dp] = gh
         ahead, behind = side_by_side(gh)
-        taps[0, WW:WW + pos] = ahead
-        taps[1, WW:WW + pos] = gh
-        taps[2, WW:WW + pos] = behind
-        back = jnp.zeros((pos, width), jnp.float32)
-        for dr in range(3):
-            start = WW - WW * (dr - 1)
-            for dc in range(3):
-                back = back + jnp.dot(
-                    taps[dc, start:start + pos], w_diag[b, 3 * dr + dc],
-                    preferred_element_type=jnp.float32,
-                )
+        sides = []
+        for h in range(2):
+            side = slice(h * half, (h + 1) * half)
+            for dc, view in enumerate((ahead, gh, behind)):
+                taps[h, dc, WW:WW + pos] = view[:, side]
+            back = jnp.zeros((pos, half), jnp.float32)
+            for dr in range(3):
+                start = WW - WW * (dr - 1)
+                for dc in range(3):
+                    back = back + jnp.dot(
+                        taps[h, dc, start:start + pos], w_diag[b, 3 * dr + dc, h],
+                        preferred_element_type=jnp.float32,
+                    )
+            sides.append(back)
+        back = jnp.concatenate(sides, axis=1)
         branch = back.astype(jnp.bfloat16).astype(jnp.float32)
         return (g_all[b, dp, me].astype(jnp.float32) + branch).astype(jnp.bfloat16)
 
@@ -278,8 +297,11 @@
                 for q in range(0, width, GS):
                     conv[b, q:q + GS, at:at + GS] = square[q:q + GS, q:q + GS]
 
-    act_all[dp] = act[...]
-    x_all[dp] = saved[...]
+    down = lax.broadcasted_iota(jnp.int32, (width, width), 0)
+    across = lax.broadcasted_iota(jnp.int32, (width, width), 1)
+    same[...] = jnp.where(lax.div(down, GS) == lax.div(across, GS), 1.0, 0.0)
+    saved[0] = in_one[...]
+    saved[1] = in_two[...]
     taps[...] = jnp.zeros_like(taps)
     entering = g_all.at[1, dp]
     middle = g_all.at[0, dp]
@@ -288,15 +310,15 @@
     def _():
         entering[:, pl.ds(pl.multiple_of(me * part, part), part)] = gtop[...]
         started = gather_start(strip(entering), 1)
+        norm_forward(1)
         spread_taps(1)
         gather_finish(strip(entering), 1, started)
-        swap_start(0, act, act_all)
-        swap_start(1, saved, x_all)
 
     @pl.when(seg < segments - 1)
     def _():
-        swap_start(0, act, act_all)
-        swap_start(1, saved, x_all)
+        norm_forward(1)
+        norm_forward(0)
+        inputs_start()
         spread_taps(1)
         spread_taps(0)
         spread_inputs()
@@ -310,7 +332,9 @@
 
     @pl.when(top_seg)
     def _():
+        norm_forward(0)
         spread_taps(0)
+        inputs_start()
 
     gather_finish(whole(middle), 0, started)
     far_start(0)
@@ -379,13 +403,6 @@
     f32 = jnp.float32
 
     top = grad_top.reshape(n_chan, width, part).swapaxes(1, 2)
-    pre = jnp.concatenate((conv_one[0], conv_two[0]), axis=0)
-    pre_t = jnp.swapaxes(pre, 1, 2).astype(f32)
-    normed, slope, inv_std, act = jax.vmap(norm_forward)(pre_t, norm_gain[0], norm_bias[0])
-    act = jnp.swapaxes(act, 1, 2)
-    saved = jnp.swapaxes(jnp.concatenate((inputs_one[0], inputs_two[0]), axis=0), 1, 2)
-    lane = jnp.arange(width)
-    same = ((lane[:, None] // GS) == (lane[None, :] // GS)).astype(f32)
     w_proj = proj_weight[0]
     proj_shape = (2, width, chans)
     if width % 128:
@@ -404,20 +421,27 @@
             jax.ShapeDtypeStruct((2, width, 9 * GS), f32),
             jax.ShapeDtypeStruct((2, 2, width), f32),
         ),
-        in_specs=[vmem] * 10,
+        in_specs=[vmem] * 9,
         out_specs=(vmem,) * 4,
         scratch_shapes=[
             pltpu.VMEM((2, n_dp, n_chan, pos, width), bf),
             pltpu.VMEM((2, n_dp, pos, width), bf),
             pltpu.VMEM((n_dp, 2, width, pos), bf),
-            pltpu.VMEM((n_dp, 2, pos, width), bf),
+            pltpu.VMEM((n_dp, 2, width, pos), bf),
             pltpu.VMEM((n_dp, 2, 2, width), f32),
             pltpu.VMEM((pos, width), bf),
-            pltpu.VMEM((3, pos + 2 * WW, width), bf),
+            pltpu.VMEM((2, 3, pos + 2 * WW, width // 2), bf),
             pltpu.VMEM((2, n_dp, 3, pos + 2 * WW, width), bf),
-            pltpu.VMEM((2, 9, width, width), bf),
+            pltpu.VMEM((2, 9, 2, width // 2, width // 2), bf),
             pltpu.VMEM((n_dp, width, pos), bf),
             pltpu.VMEM((width, width), f32),
+            pltpu.VMEM((width, width), f32),
+            pltpu.VMEM((2, pos, width), f32),
+            pltpu.VMEM((2, pos, width), f32),
+            pltpu.VMEM((2, 1, width), f32),
+            pltpu.VMEM((2, width, pos), bf),
+            pltpu.VMEM((2, width, pos), bf),
+            pltpu.VMEM((2, n_chan, width, width), bf),
             dma((2, n_chan)),
             dma((2, n_chan)),
             dma,
@@ -433,7 +457,10 @@
         compiler_params=pltpu.CompilerParams(
             collective_id=0, has_side_effects=True, vmem_limit_bytes=60 * 1024 * 1024
         ),
-    )(top, w_proj, conv_weight[0], same, slope, normed, norm_gain[0][:, None], inv_std, act, saved)
+    )(
+        top, w_proj, conv_weight[0], norm_gain[0], norm_bias[0],
+        conv_one[0, 0], conv_two[0, 0], inputs_one[0, 0], inputs_two[0, 0],
+    )
 
     latent = jnp.swapaxes(latent, 1, 2).reshape(1, 1, chans, part)
     if width % 128:

time: 155 us -> 139 us (0.90)
  other arithmetic: 6.35 us -> 0 us
  local copies, waits for them, and re-layouts: 21.3 us -> 15.4 us
  Pallas kernels: 127 us -> 122 us
    pallas_call x1, Pallas kernels: 127 us -> 122 us  [per_device(): pl.pallas_call(functools.partial(chain_kernel, segments, n_chan, n_dp), o...]
    reduce_sum x4 -> x0, other arithmetic: 2.79 us -> none  [the longest x2 1.42 us: norm_forward(): varied = jnp.mean(jnp.square(grid - centre), axis=(0, 2), keepdims=True)]
    mul x2 -> x0, local copies, waits for them, and re-layouts: 2.31 us -> none  [the longest x1 1.16 us: norm_forward(): normed = (pre_t - spread(centre)) * inv_std]
    convert_element_type x2 -> x0, other arithmetic: 2.18 us -> none  [the longest x1 1.25 us: norm_forward(): act = (scaled * gate).astype(jnp.bfloat16)]
    unnamed x17 -> x5, local copies, waits for them, and re-layouts: 12.3 us -> 11.2 us
where the time goes in v3:
time: 139 us; the launch traced here: 138 us
  Pallas kernels  122 us (88%)
  local copies, waits for them, and re-layouts  15.4 us (11%)
    pallas_call x1, Pallas kernels, per_device(): pl.pallas_call(functools.partial(chain_kernel, segments, n_chan, n_dp), o...  122 us
    unnamed x5, local copies, waits for them, and re-layouts  11.2 us

profile of v3, /device:TPU:0, one launch (start us, length us, event | category | flops | bytes accessed | tf_op | source)
XLA Modules:
  0.0 138.4 jit_solution(18361239505547453045)
XLA Ops:
  0.6 1.0 reshape.16
  1.6 0.7 copy.25
  2.3 2.2 %copy.19 = bf16[1,2,384,432]{3,2,1,0:T(8,128)(2,1)} copy(bf16[1,2,384,432]{2,3,1,0:T(8,128)(2,1)} %param.15) | data formatting | bytes 1327104 | tf_op args[6]
  4.6 122.3 %shard_map.128 = (bf16[4,64,384]{2,1,0:T(8,128)(2,1)}, f32[2,384,1536]{2,1,0:T(8,128)}, f32[2,384,432]{2,1,0:T(8,128)}, f32[2,2,384]{2,1,0:T(2,128)}) custom-call(bf16[4,64,384]{2,1,0:T(8,128)(2,1)} %bitcast.26, bf16[2,384,1536]{2,1,0:T(8,128)(2,1)} %bitcast.24, bf16[2,384,432]{2,1,0:T(8,128)(2,1)} %bitcast.23, f32[2,384]{1,0:T(2,128)} %bitcast.32, ...), custom_call_target="tpu_custom_call" | custom-call | tf_op jit(solution)/shard_map/pallas_call | solution.py:416
  126.8 1.1 copy.20
  127.9 0.8 reshape.17
  128.7 0.8 slice_bitcast_fusion
  129.4 0.6 copy.23
  130.0 0.6 copy.22
  130.6 2.9 %copy.21 = f32[1,2,384,432]{2,3,1,0:T(8,128)} copy(f32[1,2,384,432]{3,2,1,0:T(8,128)} %bitcast.25) | data formatting | bytes 2654208
  133.5 4.8 %copy.27 = f32[1,2,384,1536]{3,2,1,0:T(8,128)} copy(f32[1,2,384,1536]{3,2,1,0:T(8,128)} %bitcast.22) | data formatting | bytes 9437184

commit v4 on v3

--- a/solution.py
+++ b/solution.py
@@ -10,6 +10,7 @@
 GS = 48
 WW = 64
 NORM_EPS = 1e-05
+CUTS = 4
 MESH = pl.DeviceIdType.MESH
 
 
@@ -18,7 +19,7 @@
     latent, proj, conv, sums,
     g_all, gh_all, act_all, x_all, sums_all, last, taps, x_taps, w_diag, gh_turned, square,
     same, slope, normed, inv_std, act, saved, w_turned,
-    send_sems, recv_sems, relay_send, relay_recv, dp_send, dp_recv,
+    send_sems, recv_sems, relay_send, relay_recv, cut_send, cut_recv, dp_send, dp_recv,
     far_send, far_recv, hop_send, lat_send, lat_recv,
 ):
     seg = lax.axis_index("segment")
@@ -89,15 +90,52 @@
         for copy in started:
             copy.wait_send()
 
-    def relay():
+    def rows(i):
+        return pl.ds(i * (pos // CUTS), pos // CUTS)
+
+    def relay(i):
         return pltpu.make_async_remote_copy(
-            src_ref=last,
-            dst_ref=g_all.at[1, dp, me],
-            send_sem=relay_send,
-            recv_sem=relay_recv,
+            src_ref=last.at[rows(i)],
+            dst_ref=g_all.at[1, dp, me, rows(i)],
+            send_sem=relay_send.at[i],
+            recv_sem=relay_recv.at[i],
             device_id={"segment": lax.rem(seg + segments - 1, segments)},
             device_id_type=MESH,
         )
+
+    def cut_push(i, slot, piece, target):
+        view = g_all.at[1, dp, piece, rows(i)]
+        return pltpu.make_async_remote_copy(
+            src_ref=view,
+            dst_ref=view,
+            send_sem=cut_send.at[slot, i],
+            recv_sem=cut_recv.at[piece, i],
+            device_id={"chan": target},
+            device_id_type=MESH,
+        )
+
+    def relay_gather():
+        started = []
+        for i in range(CUTS):
+            relay(i).wait_recv()
+            copies = [cut_push(i, 1 + d, me, peer) for d, peer in enumerate(peers)]
+            copies.append(cut_push(i, 0, me, sibling))
+            for copy in copies:
+                copy.start()
+            started += copies
+        for i in range(CUTS):
+            for d, peer in enumerate(peers):
+                cut_push(i, 1 + d, peer, peer).wait_recv()
+                onward = cut_push(i, chips + d, peer, sibling)
+                onward.start()
+                started.append(onward)
+        for i in range(CUTS):
+            cut_push(i, 0, sibling, sibling).wait_recv()
+            for d in range(1, chips):
+                piece = lax.rem(row + d, chips) * 2 + 1 - core
+                cut_push(i, 0, piece, sibling).wait_recv()
+        for copy in started:
+            copy.wait_send()
 
     def swap(kind, d, src, dst):
         target = replicas[d]
@@ -322,8 +360,7 @@
         spread_taps(1)
         spread_taps(0)
         spread_inputs()
-        relay().wait_recv()
-        gather_finish(whole(entering), 1, gather_start(whole(entering), 1))
+        relay_gather()
 
     far_start(1)
     middle[me] = block(1)
@@ -342,7 +379,8 @@
 
     @pl.when(seg > 0)
     def _():
-        relay().start()
+        for i in range(CUTS):
+            relay(i).start()
 
     swap_start(3, gh_all.at[0, dp], gh_all.at[0])
     swap_start(4, sums_all.at[dp], sums_all)
@@ -388,7 +426,8 @@
 
     @pl.when(seg > 0)
     def _():
-        relay().wait_send()
+        for i in range(CUTS):
+            relay(i).wait_send()
 
 
 def per_device(
@@ -444,8 +483,10 @@
             pltpu.VMEM((2, n_chan, width, width), bf),
             dma((2, n_chan)),
             dma((2, n_chan)),
-            dma,
-            dma,
+            dma((CUTS,)),
+            dma((CUTS,)),
+            dma((n_chan, CUTS)),
+            dma((n_chan, CUTS)),
             dma((5, apart)),
             dma((5, n_dp)),
             dma((2, apart, chips)),

time: 139 us -> 131 us (0.942)
  Pallas kernels: 122 us -> 115 us
    pallas_call x1, Pallas kernels: 122 us -> 115 us  [per_device(): pl.pallas_call(functools.partial(chain_kernel, segments, n_chan, n_dp), o...]
where the time goes in v4:
time: 131 us
  Pallas kernels  115 us (88%)
  local copies, waits for them, and re-layouts  15.4 us (12%)
    pallas_call x1, Pallas kernels, per_device(): pl.pallas_call(functools.partial(chain_kernel, segments, n_chan, n_dp), o...  115 us
    unnamed x5, local copies, waits for them, and re-layouts  11.2 us

profile of v4, /device:TPU:0, one launch (start us, length us, event | category | flops | bytes accessed | tf_op | source)
XLA Modules:
  0.0 130.8 jit_solution(18215783575917843470)
XLA Ops:
  0.6 1.0 reshape.16
  1.6 0.7 copy.25
  2.3 2.2 %copy.19 = bf16[1,2,384,432]{3,2,1,0:T(8,128)(2,1)} copy(bf16[1,2,384,432]{2,3,1,0:T(8,128)(2,1)} %param.15) | data formatting | bytes 1327104 | tf_op args[6]
  4.6 114.7 %shard_map.128 = (bf16[4,64,384]{2,1,0:T(8,128)(2,1)}, f32[2,384,1536]{2,1,0:T(8,128)}, f32[2,384,432]{2,1,0:T(8,128)}, f32[2,2,384]{2,1,0:T(2,128)}) custom-call(bf16[4,64,384]{2,1,0:T(8,128)(2,1)} %bitcast.26, bf16[2,384,1536]{2,1,0:T(8,128)(2,1)} %bitcast.24, bf16[2,384,432]{2,1,0:T(8,128)(2,1)} %bitcast.23, f32[2,384]{1,0:T(2,128)} %bitcast.32, ...), custom_call_target="tpu_custom_call" | custom-call | tf_op jit(solution)/shard_map/pallas_call | solution.py:455
  119.2 1.1 copy.20
  120.3 0.8 reshape.17
  121.1 0.8 slice_bitcast_fusion
  121.8 0.6 copy.23
  122.4 0.6 copy.22
  123.0 2.9 %copy.21 = f32[1,2,384,432]{2,3,1,0:T(8,128)} copy(f32[1,2,384,432]{3,2,1,0:T(8,128)} %bitcast.25) | data formatting | bytes 2654208
  125.9 4.8 %copy.27 = f32[1,2,384,1536]{3,2,1,0:T(8,128)} copy(f32[1,2,384,1536]{3,2,1,0:T(8,128)} %bitcast.22) | data formatting | bytes 9437184
